TPU v7x, 128 devices: a whole 4x4x4 slice. The times are simulated.
128 devices in a mesh: lat: 4 (over y), lon: 32 (over x, z, core).
Axes of the slice: x: 4, y: 4, z: 4, core: 2. Of those that a mesh axis runs over, the one named last changes fastest.
Arguments:
- footprints: bfloat16 [1536, 12, 128, 512], P(('lat', 'lon')), may hold values from -0.25 to 0.25
- tile_lists: int32 [1536, 12], P(('lat', 'lon')), may hold values from 0 to 16383, as said below
- tile_counts: int32 [1536], P(('lat', 'lon')), may hold values from 6 to 12
- tile_place: int32 [16384], replicated, may hold values from 0 to 16383, as said below
- probes: float32 [1536, 8, 128], P(('lat', 'lon')), may hold values from -6 to 6
- obs_precision: float32 [1536, 128], P(('lat', 'lon')), may hold values from 0.2 to 5
- prior_sigma: float32 [1024, 2048], P('lat', 'lon'), may hold values from 0.3 to 3
- land_mask: int32 [1024, 2048], P('lat', 'lon'), may hold values 0 or 1
Outputs:
- predicted: float32 [1536, 8, 128], P(('lat', 'lon'))
- increment: float32 [1024, 32, 2048], P('lat', None, 'lon')
Inputs may be any that keep to these rules, and one draw needn't show every extreme that they name: `tile_lists`: slots j >= tile_counts[g] are padding and are ignored. Grid tile t is held by the device at lat (t // 128) // 32, lon (t % 128) // 4. At most 2 live slots of one device's groups name tiles held by any one device, and one designated device's tiles are named by exactly 2 live slots of every device's groups. `tile_place`: A permutation.
All inputs are finite; a program needn't handle non-finite values. No bound on the sum of `land_mask` on one device may be relied on, other than what follows from the above.
Results may differ from a plain program's by a relative error of at most 0.0034.
Values may be sent and summed in bfloat16 or wider, within the bound.
No kernel may reach another device: no remote copies, remote signals or barrier semaphores. Data moves between devices by JAX's collectives and lax.ppermute only.
A program may use at most 128 MiB of HBM per device.

v0:
```python
import functools

import jax
import jax.numpy as jnp
import numpy as np
from jax import lax
from jax.experimental import pallas as pl
from jax.experimental.pallas import tpu as pltpu
from jax.sharding import PartitionSpec as P

TILE_ROWS = 8
TILE_COLS = 16
WEEKS = 4
PROBES = 8
NSTEP = 4
CELLS = 128
SLOT_ROWS = WEEKS * PROBES
DOWN = 32
ACROSS = 4
TILES = DOWN * ACROSS

diffusion_rate = 0.2
week_decay = 0.6
MIB = 1 << 20

STEP_FACTOR = diffusion_rate**NSTEP


def stencil_coefficients():
    out = np.zeros((9, 9), np.int64)
    out[4, 4] = 1
    for _ in range(NSTEP):
        padded = np.pad(out, 1)
        out = (
            padded[1:-1, 1:-1]
            + padded[2:, 1:-1]
            + padded[:-2, 1:-1]
            + padded[1:-1, 2:]
            + padded[1:-1, :-2]
        )
    return out


def stencil_weights():
    coef = stencil_coefficients()
    lane = np.arange(128)
    r, c = lane // 16, lane % 16
    rows_own = r
    rows_ns = np.where(r < 4, 8 + r, r - 8)
    cols_ew = np.where(c < 8, 32 + c, c - 16)
    row_in = np.concatenate([rows_own] * 3 + [rows_ns] * 3)
    col_in = np.concatenate([c, 16 + c, cols_ew] * 2)
    row_out = np.concatenate([r, r])
    col_out = np.concatenate([c, 16 + c])
    dr = row_in[:, None] - row_out[None, :]
    dc = col_in[:, None] - col_out[None, :]
    near = (np.abs(dr) <= 4) & (np.abs(dc) <= 4)
    return np.where(near, coef[np.clip(dr + 4, 0, 8), np.clip(dc + 4, 0, 8)], 0).astype(np.float32)


def reflections():
    out = np.zeros((4, 128, 128), np.float32)
    for k in range(1, 4):
        for c in range(16):
            out[0, (k - 1) * 16 + c, (7 - k) * 16 + c] = -1
            out[1, (8 - k) * 16 + c, k * 16 + c] = -1
        for r in range(8):
            out[2, r * 16 + k - 1, r * 16 + 15 - k] = -1
            out[3, r * 16 + 16 - k, r * 16 + k] = -1
    return out


def adjoint_kernel(tile_ref, count_ref, probe_ref, prec_ref, foot_ref, out_ref, table_ref, pos_ref, seen_ref):
    g = pl.program_id(0)
    slots = foot_ref.shape[1]

    @pl.when(g == 0)
    def _():
        def clear(i, carry):
            table_ref[2 * i] = TILES
            table_ref[2 * i + 1] = TILES
            seen_ref[i] = 0
            return carry

        lax.fori_loop(0, 128, clear, 0, unroll=8)

    weighted = (prec_ref[pl.ds(g, 1), :] * probe_ref[0]).astype(jnp.bfloat16)
    count = count_ref[g]

    def slot(j):
        t = tile_ref[g * slots + j]
        row = lax.shift_right_logical(t, 7)
        col = jnp.bitwise_and(t, 127)
        owner = lax.shift_right_logical(row, 5) * 32 + lax.shift_right_logical(col, 2)
        local = jnp.bitwise_and(col, 3) * DOWN + jnp.bitwise_and(row, 31)
        rank = jnp.minimum(seen_ref[owner], 1)
        seen_ref[owner] = rank + 1
        place = owner * 2 + rank
        table_ref[place] = local
        pos_ref[g * slots + j] = place
        part = jnp.dot(weighted, foot_ref[0, j], preferred_element_type=jnp.float32)
        part = jnp.concatenate([part[:, w * CELLS : (w + 1) * CELLS] for w in range(WEEKS)], axis=0)
        out_ref[owner, pl.ds(pl.multiple_of(rank * SLOT_ROWS, SLOT_ROWS), SLOT_ROWS), :] = part.astype(jnp.bfloat16)

    for j in range(slots):
        if j < 6:
            slot(j)
        else:

            @pl.when(j < count)
            def _():
                slot(j)

            @pl.when(j >= count)
            def _():
                pos_ref[g * slots + j] = 0


def adjoint_call(grid_tile, counts, probes, precision, footprints):
    groups, slots, sounds, span = footprints.shape
    return pl.pallas_call(
        adjoint_kernel,
        out_shape=(
            jax.ShapeDtypeStruct((128, 2 * SLOT_ROWS, CELLS), jnp.bfloat16),
            jax.ShapeDtypeStruct((256,), jnp.int32),
            jax.ShapeDtypeStruct((groups * slots,), jnp.int32),
        ),
        grid=(groups,),
        in_specs=[
            pl.BlockSpec(memory_space=pltpu.SMEM),
            pl.BlockSpec(memory_space=pltpu.SMEM),
            pl.BlockSpec((1, PROBES, sounds), lambda g: (g, 0, 0)),
            pl.BlockSpec((groups, sounds), lambda g: (0, 0)),
            pl.BlockSpec((1, slots, sounds, span), lambda g: (g, 0, 0, 0)),
        ],
        out_specs=(
            pl.BlockSpec((128, 2 * SLOT_ROWS, CELLS), lambda g: (0, 0, 0)),
            pl.BlockSpec(memory_space=pltpu.SMEM),
            pl.BlockSpec(memory_space=pltpu.SMEM),
        ),
        scratch_shapes=[pltpu.SMEM((128,), jnp.int32)],
        compiler_params=pltpu.CompilerParams(vmem_limit_bytes=24 * MIB),
        name="adjoint",
    )(grid_tile, counts, probes, precision, footprints)


def receive_kernel(idx_ref, arr_ref, scale_ref, hi_ref, lo_ref, acc_a, acc_b):
    zero = jnp.zeros((SLOT_ROWS, CELLS), jnp.float32)

    def clear(i, carry):
        acc_a[i] = zero
        acc_b[i] = zero
        return carry

    lax.fori_loop(0, TILES, clear, 0, unroll=8)

    def add(d, carry):
        ia = idx_ref[2 * d]
        ib = idx_ref[2 * d + 1]
        acc_a[ia] += arr_ref[d, :SLOT_ROWS, :].astype(jnp.float32)
        acc_b[ib] += arr_ref[d, SLOT_ROWS:, :].astype(jnp.float32)
        return carry

    lax.fori_loop(0, 128, add, 0, unroll=4)

    for tc in range(ACROSS):

        def finish(tr, carry):
            t = tc * DOWN + tr
            x = [acc_a[t, w * 8 : w * 8 + 8, :] + acc_b[t, w * 8 : w * 8 + 8, :] for w in range(WEEKS)]
            scale = scale_ref[tc, pl.ds(tr, 1), :]
            ahead = [x[0]]
            for w in range(1, WEEKS):
                ahead.append(x[w] + week_decay * ahead[-1])
            mixed = [None] * WEEKS
            mixed[WEEKS - 1] = ahead[WEEKS - 1]
            behind = week_decay * x[WEEKS - 1]
            for w in range(WEEKS - 2, -1, -1):
                mixed[w] = ahead[w] + behind
                behind = week_decay * (x[w] + behind)
            y = jnp.concatenate(mixed, axis=0) * scale
            hi = y.astype(jnp.bfloat16)
            hi_ref[tc, tr] = hi
            lo_ref[tc, tr] = (y - hi.astype(jnp.float32)).astype(jnp.bfloat16)
            return carry

        lax.fori_loop(0, DOWN, finish, 0, unroll=4)


def receive_call(index, arrived, scale):
    shape = jax.ShapeDtypeStruct((ACROSS, DOWN, SLOT_ROWS, CELLS), jnp.bfloat16)
    return pl.pallas_call(
        receive_kernel,
        out_shape=(shape, shape),
        in_specs=[
            pl.BlockSpec(memory_space=pltpu.SMEM),
            pl.BlockSpec(memory_space=pltpu.VMEM),
            pl.BlockSpec(memory_space=pltpu.VMEM),
        ],
        out_specs=(pl.BlockSpec(memory_space=pltpu.VMEM),) * 2,
        scratch_shapes=[
            pltpu.VMEM((TILES + 1, SLOT_ROWS, CELLS), jnp.float32),
            pltpu.VMEM((TILES + 1, SLOT_ROWS, CELLS), jnp.float32),
        ],
        compiler_params=pltpu.CompilerParams(vmem_limit_bytes=24 * MIB),
        name="receive",
    )(index, arrived, scale)


def diffuse_kernel(
    where_ref, idx_ref, hi_ref, lo_ref, north_ref, south_ref, west_ref, east_ref, scale_ref, weight_ref, mirror_ref,
    inc_ref, reply_ref, half_ref, nh, sh, wh, eh, left_ref,
):
    lat, lon = where_ref[0], where_ref[1]
    flat = (SLOT_ROWS, CELLS)

    def mirrored(block, side):
        rows = block.reshape(-1, CELLS)
        out = jnp.dot(rows, mirror_ref[side], preferred_element_type=jnp.float32)
        return out.astype(jnp.bfloat16).reshape(block.shape)

    nh[...] = north_ref[...]
    sh[...] = south_ref[...]
    wh[...] = west_ref[...]
    eh[...] = east_ref[...]

    @pl.when(lat == 0)
    def _():
        for tc in range(ACROSS):
            nh[tc] = mirrored(hi_ref[tc, 0], 0)

    @pl.when(lat == 3)
    def _():
        for tc in range(ACROSS):
            sh[tc] = mirrored(hi_ref[tc, DOWN - 1], 1)

    @pl.when(lon == 0)
    def _():
        wh[0] = mirrored(nh[0], 2)
        wh[1 : DOWN + 1] = mirrored(hi_ref[0], 2)
        wh[DOWN + 1] = mirrored(sh[0], 2)

    @pl.when(lon == 31)
    def _():
        eh[0] = mirrored(nh[ACROSS - 1], 3)
        eh[1 : DOWN + 1] = mirrored(hi_ref[ACROSS - 1], 3)
        eh[DOWN + 1] = mirrored(sh[ACROSS - 1], 3)

    @pl.when(lat == 0)
    def _():
        wh[0] = mirrored(wh[1], 0)
        eh[0] = mirrored(eh[1], 0)

    @pl.when(lat == 3)
    def _():
        wh[DOWN + 1] = mirrored(wh[DOWN], 1)
        eh[DOWN + 1] = mirrored(eh[DOWN], 1)

    lane = lax.broadcasted_iota(jnp.int32, flat, 1)
    upper = lane < 64
    east_side = jnp.bitwise_and(lane, 15) < 8
    chunk = 8
    zero = jnp.zeros(flat, jnp.bfloat16)

    for pair in range(ACROSS // 2):
        for part in range(DOWN // chunk):
            total = None
            for ref, is_hi in ((hi_ref, True), (lo_ref, False)):

                def tile(x, tr):
                    if x < 0 or x >= ACROSS:
                        if not is_hi:
                            return zero
                        return (wh if x < 0 else eh)[tr + 1]
                    if tr < 0 or tr >= DOWN:
                        if not is_hi:
                            return zero
                        return (nh if tr < 0 else sh)[x]
                    return ref[x, tr]

                for k in range(chunk):
                    tr = part * chunk + k
                    own, both = [], []
                    for x in range(2 * pair - 1, 2 * pair + 3):
                        own.append(tile(x, tr))
                        both.append(jnp.where(upper, tile(x, tr + 1), tile(x, tr - 1)))
                    rows = slice(k * SLOT_ROWS, (k + 1) * SLOT_ROWS)
                    left_ref[rows, 0:128] = own[1]
                    left_ref[rows, 128:256] = own[2]
                    left_ref[rows, 256:384] = jnp.where(east_side, own[3], own[0])
                    left_ref[rows, 384:512] = both[1]
                    left_ref[rows, 512:640] = both[2]
                    left_ref[rows, 640:768] = jnp.where(east_side, both[3], both[0])
                product = jnp.dot(left_ref[...], weight_ref[...], preferred_element_type=jnp.float32)
                total = product if total is None else total + product
            for k in range(chunk):
                tr = part * chunk + k
                for u in range(2):
                    tc = 2 * pair + u
                    scale = scale_ref[tc, tr : tr + 1, :] * STEP_FACTOR
                    y = total[k * SLOT_ROWS : (k + 1) * SLOT_ROWS, u * 128 : (u + 1) * 128] * scale
                    inc_ref[tc, tr] = y
                    half_ref[tc * DOWN + tr] = y.astype(jnp.bfloat16)

    def answer(d, carry):
        reply_ref[d, :SLOT_ROWS, :] = half_ref[idx_ref[2 * d]]
        reply_ref[d, SLOT_ROWS:, :] = half_ref[idx_ref[2 * d + 1]]
        return carry

    lax.fori_loop(0, 128, answer, 0, unroll=8)


def diffuse_call(where, index, hi, lo, north, south, west, east, scale, weight, mirror):
    vmem = pl.BlockSpec(memory_space=pltpu.VMEM)
    smem = pl.BlockSpec(memory_space=pltpu.SMEM)
    return pl.pallas_call(
        diffuse_kernel,
        out_shape=(
            jax.ShapeDtypeStruct((ACROSS, DOWN, SLOT_ROWS, CELLS), jnp.float32),
            jax.ShapeDtypeStruct((128, 2 * SLOT_ROWS, CELLS), jnp.bfloat16),
        ),
        in_specs=[smem, smem] + [vmem] * 9,
        out_specs=(vmem, vmem),
        scratch_shapes=[
            pltpu.VMEM((TILES + 1, SLOT_ROWS, CELLS), jnp.bfloat16),
            pltpu.VMEM((ACROSS, SLOT_ROWS, CELLS), jnp.bfloat16),
            pltpu.VMEM((ACROSS, SLOT_ROWS, CELLS), jnp.bfloat16),
            pltpu.VMEM((DOWN + 2, SLOT_ROWS, CELLS), jnp.bfloat16),
            pltpu.VMEM((DOWN + 2, SLOT_ROWS, CELLS), jnp.bfloat16),
            pltpu.VMEM((8 * SLOT_ROWS, 768), jnp.bfloat16),
        ],
        compiler_params=pltpu.CompilerParams(vmem_limit_bytes=32 * MIB),
        name="diffuse",
    )(where, index, hi, lo, north, south, west, east, scale, weight, mirror)


def layout_kernel(inc_ref, out_ref, rows_ref):
    lane = lax.broadcasted_iota(jnp.int32, (8, CELLS), 1)
    group = lax.shift_right_logical(lane, 4)

    def regroup(tr, carry):
        for half in range(2):
            v = [
                inc_ref[i % 4, tr, (half * 2 + i // 4) * 8 : (half * 2 + i // 4) * 8 + 8, :] for i in range(8)
            ]
            for bit in (1, 2, 4):
                clear = jnp.bitwise_and(group, bit) == 0
                for i in range(8):
                    if i & bit == 0:
                        a, c = v[i], v[i + bit]
                        v[i] = jnp.where(clear, a, pltpu.roll(c, 16 * bit, 1))
                        v[i + bit] = jnp.where(clear, pltpu.roll(a, 128 - 16 * bit, 1), c)
            for r in range(8):
                at = pl.multiple_of((half * 256 + tr * 8 + r) * 8, 8)
                rows_ref[pl.ds(at, 8), :] = v[r]
        return carry

    lax.fori_loop(0, DOWN, regroup, 0, unroll=2)

    for half in range(2):
        for p in range(PROBES):
            for k in range(2):
                block = rows_ref[pl.ds((half * 256 + k * 128) * 8 + p, 128, stride=8), :]
                out_ref[pl.ds((p * 4 + half * 2) * 64, 128), k * 128 : (k + 1) * 128] = block.T


def layout_call(inc):
    return pl.pallas_call(
        layout_kernel,
        out_shape=jax.ShapeDtypeStruct((SLOT_ROWS * 64, 256), jnp.float32),
        in_specs=[pl.BlockSpec(memory_space=pltpu.VMEM)],
        out_specs=pl.BlockSpec(memory_space=pltpu.VMEM),
        scratch_shapes=[pltpu.VMEM((2 * 256 * 8, CELLS), jnp.float32)],
        compiler_params=pltpu.CompilerParams(vmem_limit_bytes=16 * MIB),
        cost_estimate=pl.CostEstimate(flops=8 * MIB, bytes_accessed=8 * MIB, transcendentals=0),
        name="layout",
    )(inc)


def forward_kernel(pos_ref, count_ref, tiles_ref, foot_ref, out_ref):
    g = pl.program_id(0)
    slots = foot_ref.shape[1]
    count = count_ref[g]
    total = jnp.zeros((PROBES, foot_ref.shape[2]), jnp.float32)
    for j in range(slots):
        place = pos_ref[g * slots + j]
        at = pl.multiple_of(jnp.bitwise_and(place, 1) * SLOT_ROWS, SLOT_ROWS)
        tile = tiles_ref[lax.shift_right_logical(place, 1), pl.ds(at, SLOT_ROWS), :].astype(jnp.float32)
        left = jnp.concatenate([tile[w * 8 : w * 8 + 8] for w in range(WEEKS)], axis=1).astype(jnp.bfloat16)
        value = lax.dot_general(
            left, foot_ref[0, j], (((1,), (1,)), ((), ())), preferred_element_type=jnp.float32
        )
        total = total + (value if j < 6 else jnp.where(j < count, value, 0.0))
    out_ref[0] = total


def forward_call(pos, counts, tiles, footprints):
    groups, slots, sounds, span = footprints.shape
    return pl.pallas_call(
        forward_kernel,
        out_shape=jax.ShapeDtypeStruct((groups, PROBES, sounds), jnp.float32),
        grid=(groups,),
        in_specs=[
            pl.BlockSpec(memory_space=pltpu.SMEM),
            pl.BlockSpec(memory_space=pltpu.SMEM),
            pl.BlockSpec((128, 2 * SLOT_ROWS, CELLS), lambda g: (0, 0, 0)),
            pl.BlockSpec((1, slots, sounds, span), lambda g: (g, 0, 0, 0)),
        ],
        out_specs=pl.BlockSpec((1, PROBES, sounds), lambda g: (g, 0, 0)),
        compiler_params=pltpu.CompilerParams(vmem_limit_bytes=24 * MIB),
        name="forward",
    )(pos, counts, tiles, footprints)


def exchanged(block):
    return lax.all_to_all(block, ("lat", "lon"), split_axis=0, concat_axis=0, tiled=True)


def per_device(
    footprints, tile_lists, tile_counts, tile_place, probes, obs_precision, prior_sigma, land_mask
):
    lat, lon = lax.axis_index("lat"), lax.axis_index("lon")
    me = lat * 32 + lon
    grid_tile = tile_place[tile_lists.reshape(-1)]
    outgoing, table, pos = adjoint_call(grid_tile, tile_counts, probes, obs_precision, footprints)
    arrived = exchanged(outgoing)
    tables = lax.all_gather(table, ("lat", "lon"), axis=0, tiled=False)
    index = lax.dynamic_slice(tables, (0, 2 * me), (128, 2)).reshape(256)

    scale = prior_sigma * land_mask.astype(jnp.float32)
    scale = scale.reshape(DOWN, TILE_ROWS, ACROSS, TILE_COLS).transpose(2, 0, 1, 3).reshape(ACROSS, DOWN, CELLS)

    hi, lo = receive_call(index, arrived, scale)

    south_way = [(i, i + 1) for i in range(3)]
    north_way = [(i + 1, i) for i in range(3)]
    east_way = [(i, i + 1) for i in range(31)]
    west_way = [(i + 1, i) for i in range(31)]
    north = lax.ppermute(hi[:, DOWN - 1], "lat", south_way)
    south = lax.ppermute(hi[:, 0], "lat", north_way)
    edge_w = jnp.concatenate([north[:1], hi[0], south[:1]], axis=0)
    edge_e = jnp.concatenate([north[3:], hi[ACROSS - 1], south[3:]], axis=0)
    west = lax.ppermute(edge_e, "lon", east_way)
    east = lax.ppermute(edge_w, "lon", west_way)

    where = jnp.stack([lat, lon]).astype(jnp.int32)
    weight = jnp.asarray(stencil_weights(), jnp.bfloat16)
    mirror = jnp.asarray(reflections(), jnp.bfloat16)
    inc, reply = diffuse_call(where, index, hi, lo, north, south, west, east, scale, weight, mirror)
    returned = exchanged(reply)
    increment = layout_call(inc).reshape(SLOT_ROWS, 64, 256).transpose(2, 0, 1)
    predicted = forward_call(pos, tile_counts, returned, footprints)
    return (predicted, increment)


def solution(mesh):
    in_specs = (
        P(("lat", "lon"), None, None, None),
        P(("lat", "lon"), None),
        P(("lat", "lon")),
        P(),
        P(("lat", "lon"), None, None),
        P(("lat", "lon"), None),
        P("lat", "lon"),
        P("lat", "lon"),
    )
    out_specs = (P(("lat", "lon"), None, None), P("lat", None, "lon"))
    return jax.shard_map(
        per_device, mesh=mesh, in_specs=in_specs, out_specs=out_specs, check_vma=False
    )
```

profile of v0, /device:TPU:0, one launch (start us, length us, event | category | flops | bytes accessed | tf_op | source)
XLA Modules:
  0.0 169.1 jit_solution(9300831268348452692)
XLA Ops:
  0.6 0.0 copy-start
  0.6 0.8 reshape.47
  1.5 0.0 copy-done
  1.5 1.4 gather_fusion
  2.9 0.0 copy-start.1
  3.0 6.4 %copy-done.1 = bf16[12,12,128,512]{3,2,1,0:T(8,128)(2,1)S(1)} copy-done((bf16[12,12,128,512]{3,2,1,0:T(8,128)(2,1)S(1)}, bf16[12,12,128,512]{3,2,1,0:T(8,128)(2,1)}, u32[]{:S(2)}) %copy-start.1) | copy-done | bytes 18874392
  9.3 0.8 copy-done.9
  10.1 0.7 copy-done.10
  10.8 0.7 copy-done.11
  11.5 8.3 %adjoint.1 = (bf16[128,64,128]{2,1,0:T(8,128)(2,1)S(1)}, s32[256]{0:T(256)S(1)}, s32[144]{0:T(256)S(1)}) custom-call(s32[144]{0:T(256)S(1)} %gather_fusion, s32[12]{0:T(128)S(1)} %copy-done.11, f32[12,8,128]{2,1,0:T(8,128)S(1)} %copy-done.9, f32[12,128]{1,0:T(8,128)S(1)} %copy-done.10, bf16[12,12,128,512]{3,2,1,0:T(8,128)(2,1)S(1)} %copy-done.1), custom_call_target="tpu_custom_call" | custom-call | tf_op jit(solution)/shard_map/adjoint/pallas_call | solution.py:121
  19.8 0.0 copy-start.3
  19.8 1.3 copy-done.3
  21.1 12.1 %all-to-all-start = ((bf16[128,64,128]{2,1,0:T(8,128)(2,1)}), bf16[128,64,128]{2,1,0:T(8,128)(2,1)S(1)}, u32[]{:S(2)}, u32[]{:S(2)}) async-start(bf16[128,64,128]{2,1,0:T(8,128)(2,1)} %copy-done.3), calls=%async_computation | async-start | bytes 4194304 | tf_op jit(solution)/shard_map/all_to_all | solution.py:416
  33.2 0.0 copy-done.13
  33.2 0.0 copy-done.14
  33.2 0.1 copy.21
  33.3 0.3 reshape.49
  33.6 0.3 copy.22
  34.0 0.1 copy.23.scale_ref
  34.1 52.4 %all-gather.1 = s32[128,1,256]{2,1,0:T(1,128)S(1)} all-gather(s32[1,1,256]{2,1,0:T(1,128)S(1)} %bitcast.17), channel_id=2, replica_groups=mesh['lat'=4,'lon'=32] {'lat','lon'}, dimensions={0}, use_global_device_ids=true | all-gather | bytes 132096 | tf_op jit(solution)/shard_map/all_gather | solution.py:427
  86.5 0.2 dynamic-slice_reduce_fusion
  86.7 0.1 reshape.48.idx_ref
  86.9 0.0 copy-start.7
  86.9 0.0 copy-start.8
  86.9 0.0 all-to-all-done.arr_ref
  86.9 2.6 %receive.1 = (bf16[4,32,32,128]{3,2,1,0:T(8,128)(2,1)S(1)}, bf16[4,32,32,128]{3,2,1,0:T(8,128)(2,1)S(1)}) custom-call(s32[256]{0:T(256)S(1)} %reshape.48.idx_ref, bf16[128,64,128]{2,1,0:T(8,128)(2,1)S(1)} %all-to-all-done.arr_ref, f32[4,32,128]{2,1,0:T(8,128)S(1)} %copy.23.scale_ref), custom_call_target="tpu_custom_call" | custom-call | tf_op jit(solution)/shard_map/receive/pallas_call | solution.py:192
  89.5 1.3 collective-permute-start.1
  90.9 4.5 %collective-permute-start = (bf16[4,32,128]{2,1,0:T(8,128)(2,1)S(1)}, bf16[4,32,128]{2,1,0:T(8,128)(2,1)S(1)}, u32[]{:S(2)}, u32[]{:S(2)}) collective-permute-start(bf16[4,32,128]{2,1,0:T(8,128)(2,1)S(1)} %get-tuple-element.19), channel_id=1, source_target_pairs={{0,32},{32,64},{64,96},{1,33},{33,65},{65,97},{2,34},{34,66},{66,9... | collective-permute-start | bytes 98312 | tf_op jit(solution)/shard_map/ppermute | solution.py:439
  95.4 0.0 collective-permute-done.1.south_ref
  95.5 1.6 collective-permute-done.north_ref
  97.1 1.3 collective-permute-start.2
  98.4 1.3 collective-permute-start.3
  99.7 0.1 pad_add_fusion.where_ref
  99.8 0.0 collective-permute-done.2.west_ref
  99.8 2.1 %collective-permute-done.3.east_ref = bf16[34,32,128]{2,1,0:T(8,128)(2,1)S(1)} collective-permute-done((bf16[34,32,128]{2,1,0:T(8,128)(2,1)S(1)}, bf16[34,32,128]{2,1,0:T(8,128)(2,1)S(1)}, u32[]{:S(2)}, u32[]{:S(2)}) %collective-permute-start.3) | collective-permute-done | bytes 278560 | tf_op jit(solution)/shard_map/ppermute | solution.py:444
  101.9 0.0 copy-done.7
  101.9 0.0 copy-done.8
  101.9 4.6 %diffuse.1 = (f32[4,32,32,128]{3,2,1,0:T(8,128)S(1)}, bf16[128,64,128]{2,1,0:T(8,128)(2,1)S(1)}) custom-call(s32[2]{0:T(128)S(1)} %pad_add_fusion.where_ref, s32[256]{0:T(256)S(1)} %reshape.48.idx_ref, bf16[4,32,32,128]{3,2,1,0:T(8,128)(2,1)S(1)} %get-tuple-element.12.hi_ref, bf16[4,32,32,128]{3,2,1,0:T(8,128)(2,1)S(1)} %get-tuple-element.13.lo_ref, ...), custom_call_target="tpu_custom_call" | custom-call | tf_op jit(solution)/shard_map/diffuse/pallas_call | solution.py:316
  106.5 0.0 copy-start.4
  106.5 1.3 copy-done.4
  107.8 1.3 copy-done.6
  109.1 15.3 %all-to-all-start.1 = ((bf16[128,64,128]{2,1,0:T(8,128)(2,1)}), bf16[128,64,128]{2,1,0:T(8,128)(2,1)S(1)}, u32[]{:S(2)}, u32[]{:S(2)}) async-start(bf16[128,64,128]{2,1,0:T(8,128)(2,1)} %copy-done.6), calls=%async_computation.1 | async-start | bytes 4194304 | tf_op jit(solution)/shard_map/all_to_all | solution.py:416
  124.4 0.0 copy-start.5
  124.4 1.6 copy-done.5
  126.0 5.8 %layout.1 = f32[2048,256]{1,0:T(8,128)} custom-call(f32[4,32,32,128]{3,2,1,0:T(8,128)S(1)} %copy-done.5), custom_call_target="tpu_custom_call" | custom-call | flops 8388608 | bytes 8388608 | tf_op jit(solution)/shard_map/layout/pallas_call | solution.py:368
  131.9 23.0 %all-to-all-done.1.tiles_ref = bf16[128,64,128]{2,1,0:T(8,128)(2,1)S(1)} async-done(((bf16[128,64,128]{2,1,0:T(8,128)(2,1)}), bf16[128,64,128]{2,1,0:T(8,128)(2,1)S(1)}, u32[]{:S(2)}, u32[]{:S(2)}) %all-to-all-start.1) | async-done | bytes 2097184 | tf_op jit(solution)/shard_map/all_to_all | solution.py:416
  154.9 6.4 %copy-done.2 = bf16[12,12,128,512]{3,2,1,0:T(8,128)(2,1)S(1)} copy-done((bf16[12,12,128,512]{3,2,1,0:T(8,128)(2,1)S(1)}, bf16[12,12,128,512]{3,2,1,0:T(8,128)(2,1)}, u32[]{:S(2)}) %copy-start.2) | copy-done | bytes 18874392
  161.2 7.8 %forward.1 = f32[12,8,128]{2,1,0:T(8,128)} custom-call(s32[144]{0:T(256)S(1)} %get-tuple-element.9.pos_ref, s32[12]{0:T(128)S(1)} %copy-done.12, bf16[128,64,128]{2,1,0:T(8,128)(2,1)S(1)} %all-to-all-done.1.tiles_ref, bf16[12,12,128,512]{3,2,1,0:T(8,128)(2,1)S(1)} %copy-done.2), custom_call_target="tpu_custom_call" | custom-call | tf_op jit(solution)/shard_map/forward/pallas_call | solution.py:399
  (18 shorter events, 0.2 us)
Async XLA Ops:
  0.6 0.9 copy-start
  2.9 6.4 %copy-start.1 = (bf16[12,12,128,512]{3,2,1,0:T(8,128)(2,1)S(1)}, bf16[12,12,128,512]{3,2,1,0:T(8,128)(2,1)}, u32[]{:S(2)}) copy-start(bf16[12,12,128,512]{3,2,1,0:T(8,128)(2,1)} %foot_ref.3) | copy-start | bytes 56623108
  9.3 0.8 copy-start.9
  10.1 0.7 copy-start.10
  10.8 0.7 copy-start.11
  19.8 1.3 copy-start.3
  21.1 12.1 %copy-start.13 = (f32[256,64]{0,1:T(8,128)S(1)}, f32[256,64]{0,1:T(8,128)}, u32[]{:S(2)}) copy-start(f32[256,64]{0,1:T(8,128)} %param.16) | copy-start | bytes 196612
  21.1 12.1 %copy-start.14 = (s32[256,64]{0,1:T(8,128)S(1)}, s32[256,64]{0,1:T(8,128)}, u32[]{:S(2)}) copy-start(s32[256,64]{0,1:T(8,128)} %param.17) | copy-start | bytes 196612
  21.1 65.8 %all-to-all-start = ((bf16[128,64,128]{2,1,0:T(8,128)(2,1)}), bf16[128,64,128]{2,1,0:T(8,128)(2,1)S(1)}, u32[]{:S(2)}, u32[]{:S(2)}) async-start(bf16[128,64,128]{2,1,0:T(8,128)(2,1)} %copy-done.3), calls=%async_computation | async-start | bytes 4194304 | tf_op jit(solution)/shard_map/all_to_all | solution.py:416
  86.9 15.0 %copy-start.7 = (bf16[768,256]{1,0:T(8,128)(2,1)S(1)}, bf16[768,256]{1,0:T(8,128)(2,1)}, u32[]{:S(2)}) copy-start(bf16[768,256]{1,0:T(8,128)(2,1)} %constant.24.clone.weight_ref) | copy-start | bytes 1179652
  86.9 15.0 %copy-start.8 = (bf16[4,128,128]{2,1,0:T(8,128)(2,1)S(1)}, bf16[4,128,128]{2,1,0:T(8,128)(2,1)}, u32[]{:S(2)}) copy-start(bf16[4,128,128]{2,1,0:T(8,128)(2,1)} %constant.25.clone.mirror_ref) | copy-start | bytes 393220
  89.5 5.9 %collective-permute-start.1 = (bf16[4,32,128]{2,1,0:T(8,128)(2,1)S(1)}, bf16[4,32,128]{2,1,0:T(8,128)(2,1)S(1)}, u32[]{:S(2)}, u32[]{:S(2)}) collective-permute-start(bf16[4,32,128]{2,1,0:T(8,128)(2,1)S(1)} %get-tuple-element.18), channel_id=1, source_target_pairs={{32,0},{64,32},{96,64},{33,1},{65,33},{97,65},{34,2},{66,34},{98,6... | collective-permute-start | bytes 98312 | tf_op jit(solution)/shard_map/ppermute | solution.py:440
  90.9 6.1 %collective-permute-start = (bf16[4,32,128]{2,1,0:T(8,128)(2,1)S(1)}, bf16[4,32,128]{2,1,0:T(8,128)(2,1)S(1)}, u32[]{:S(2)}, u32[]{:S(2)}) collective-permute-start(bf16[4,32,128]{2,1,0:T(8,128)(2,1)S(1)} %get-tuple-element.19), channel_id=1, source_target_pairs={{0,32},{32,64},{64,96},{1,33},{33,65},{65,97},{2,34},{34,66},{66,9... | collective-permute-start | bytes 98312 | tf_op jit(solution)/shard_map/ppermute | solution.py:439
  97.1 2.7 %collective-permute-start.2 = (bf16[34,32,128]{2,1,0:T(8,128)(2,1)S(1)}, bf16[34,32,128]{2,1,0:T(8,128)(2,1)S(1)}, u32[]{:S(2)}, u32[]{:S(2)}) collective-permute-start(bf16[34,32,128]{2,1,0:T(8,128)(2,1)S(1)} %pad_maximum_fusion), channel_id=1, source_target_pairs={{0,1},{1,2},{2,3},{3,4},{4,5},{5,6},{6,7},{7,8},{8,9},{9,10},{10,1... | collective-permute-start | bytes 835592 | tf_op jit(solution)/shard_map/ppermute | solution.py:443
  98.4 3.5 %collective-permute-start.3 = (bf16[34,32,128]{2,1,0:T(8,128)(2,1)S(1)}, bf16[34,32,128]{2,1,0:T(8,128)(2,1)S(1)}, u32[]{:S(2)}, u32[]{:S(2)}) collective-permute-start(bf16[34,32,128]{2,1,0:T(8,128)(2,1)S(1)} %pad_maximum_fusion.1), channel_id=1, source_target_pairs={{1,0},{2,1},{3,2},{4,3},{5,4},{6,5},{7,6},{8,7},{9,8},{10,9},{11,1... | collective-permute-start | bytes 835592 | tf_op jit(solution)/shard_map/ppermute | solution.py:444
  106.5 1.3 copy-start.4
  107.8 1.3 copy-start.6
  109.1 45.8 %all-to-all-start.1 = ((bf16[128,64,128]{2,1,0:T(8,128)(2,1)}), bf16[128,64,128]{2,1,0:T(8,128)(2,1)S(1)}, u32[]{:S(2)}, u32[]{:S(2)}) async-start(bf16[128,64,128]{2,1,0:T(8,128)(2,1)} %copy-done.6), calls=%async_computation.1 | async-start | bytes 4194304 | tf_op jit(solution)/shard_map/all_to_all | solution.py:416
  124.4 1.6 copy-start.5
  126.0 28.8 %copy-start.12 = (s32[12]{0:T(128)S(1)}, s32[12]{0:T(128)}, u32[]{:S(2)}) copy-start(s32[12]{0:T(128)} %count_ref.3) | copy-start | bytes 148
  154.9 6.4 %copy-start.2 = (bf16[12,12,128,512]{3,2,1,0:T(8,128)(2,1)S(1)}, bf16[12,12,128,512]{3,2,1,0:T(8,128)(2,1)}, u32[]{:S(2)}) copy-start(bf16[12,12,128,512]{3,2,1,0:T(8,128)(2,1)} %foot_ref.3) | copy-start | bytes 56623108
where the time goes:
time: 170 us; the launch traced here: 169 us
  blocking collectives  52.4 us (31%)
  starting transfers between devices  35.8 us (21%)
  Pallas kernels  29.2 us (17%)
  waiting for transfers between devices  26.6 us (16%)
  local copies, waits for them, and re-layouts  23.9 us (14%)
    all_gather x1, blocking collectives, per_device(): tables = lax.all_gather(table, ('lat', 'lon'), axis=0, tiled=False)  52.4 us
    all_to_all x2, starting transfers between devices, exchanged(): lax.all_to_all(block, ('lat', 'lon'), split_axis=0, concat_axis=0, tiled=...  27.4 us
    all_to_all x2, waiting for transfers between devices, exchanged(): lax.all_to_all(block, ('lat', 'lon'), split_axis=0, concat_axis=0, tiled=...  23 us
    unnamed x30, local copies, waits for them, and re-layouts  20.5 us
    pallas_call x1, Pallas kernels, adjoint_call(): pl.pallas_call(adjoint_kernel, out_shape=(jax.ShapeDtypeStruct((128, 2 *...  8.32 us
    pallas_call x1, Pallas kernels, forward_call(): pl.pallas_call(forward_kernel, out_shape=jax.ShapeDtypeStruct((groups, PR...  7.84 us
    pallas_call x1, Pallas kernels, layout_call(): pl.pallas_call(layout_kernel, out_shape=jax.ShapeDtypeStruct((SLOT_ROWS *...  5.83 us
    pallas_call x1, Pallas kernels, diffuse_call(): pl.pallas_call(diffuse_kernel, out_shape=(jax.ShapeDtypeStruct((ACROSS, D...  4.56 us
  transfers between devices with their start and end apart: 6, of which 3 were waited for; matrix products, arithmetic and copies ran while one was open for 1% of the time, Pallas kernels for 3%

commit v1 on v0

v1 whole, which is shorter than its diff:
```python
import functools

import jax
import jax.numpy as jnp
import numpy as np
from jax import lax
from jax.experimental import pallas as pl
from jax.experimental.pallas import tpu as pltpu
from jax.sharding import PartitionSpec as P

TILE_ROWS = 8
TILE_COLS = 16
WEEKS = 4
PROBES = 8
NSTEP = 4
CELLS = 128
SLOT_ROWS = WEEKS * PROBES
DOWN = 32
ACROSS = 4
TILES = DOWN * ACROSS
SEND_ROWS = 2 * SLOT_ROWS + 8
QUADS = DOWN // 4

diffusion_rate = 0.2
week_decay = 0.6
MIB = 1 << 20

STEP_FACTOR = diffusion_rate**NSTEP


def stencil_coefficients():
    out = np.zeros((9, 9), np.int64)
    out[4, 4] = 1
    for _ in range(NSTEP):
        padded = np.pad(out, 1)
        out = (
            padded[1:-1, 1:-1]
            + padded[2:, 1:-1]
            + padded[:-2, 1:-1]
            + padded[1:-1, 2:]
            + padded[1:-1, :-2]
        )
    return out


def stencil_weights():
    coef = stencil_coefficients()
    lane = np.arange(128)
    r, c = lane // 16, lane % 16
    rows_own = r
    rows_ns = np.where(r < 4, 8 + r, r - 8)
    cols_ew = np.where(c < 8, 32 + c, c - 16)
    row_in = np.concatenate([rows_own] * 3 + [rows_ns] * 3)
    col_in = np.concatenate([c, 16 + c, cols_ew] * 2)
    row_out = np.concatenate([r, r])
    col_out = np.concatenate([c, 16 + c])
    dr = row_in[:, None] - row_out[None, :]
    dc = col_in[:, None] - col_out[None, :]
    near = (np.abs(dr) <= 4) & (np.abs(dc) <= 4)
    return np.where(near, coef[np.clip(dr + 4, 0, 8), np.clip(dc + 4, 0, 8)], 0).astype(np.float32)


def reflections():
    out = np.zeros((4, 128, 128), np.float32)
    for k in range(1, 4):
        for c in range(16):
            out[0, (k - 1) * 16 + c, (7 - k) * 16 + c] = -1
            out[1, (8 - k) * 16 + c, k * 16 + c] = -1
        for r in range(8):
            out[2, r * 16 + k - 1, r * 16 + 15 - k] = -1
            out[3, r * 16 + 16 - k, r * 16 + k] = -1
    return out


def in_hbm(x):
    return pltpu.with_memory_space_constraint(x, pltpu.HBM)


def adjoint_kernel(
    list_hbm, count_hbm, place_hbm, probe_hbm, prec_hbm, foot_hbm, out_hbm, pos_ref,
    foot, packed, probe_ref, prec_ref, list_ref, count_ref, place_ref, table_ref, seen_ref, small_sem, foot_sem, out_sem,
):
    groups, slots = foot.shape[:2]
    pairs = slots // 2
    small = [
        pltpu.make_async_copy(src, dst, small_sem.at[k])
        for k, (src, dst) in enumerate(
            (
                (count_hbm, count_ref),
                (list_hbm, list_ref),
                (place_hbm, place_ref),
                (probe_hbm, probe_ref),
                (prec_hbm, prec_ref),
            )
        )
    ]
    for copy in small:
        copy.start()

    def fetch(g, j):
        return pltpu.make_async_copy(foot_hbm.at[g, pl.ds(2 * j, 2)], foot.at[g, pl.ds(2 * j, 2)], foot_sem.at[g, j])

    def start_sure(g, carry):
        for j in range(3):
            fetch(g, j).start()
        return carry

    def start_rest(g, carry):
        count = count_ref[g]
        for j in range(3, pairs):

            @pl.when(2 * j < count)
            def _():
                fetch(g, j).start()

        return carry

    start_sure(0, 0)
    small[0].wait()
    start_rest(0, 0)

    def start_group(g, carry):
        start_sure(g, carry)
        return start_rest(g, carry)

    lax.fori_loop(1, groups, start_group, 0)

    def clear(i, carry):
        table_ref[2 * i] = TILES
        table_ref[2 * i + 1] = TILES
        seen_ref[i] = 0
        return carry

    lax.fori_loop(0, 129, clear, 0, unroll=3)
    for copy in small[1:]:
        copy.wait()

    def group(g, carry):
        count = count_ref[g]
        weighted = prec_ref[pl.ds(g, 1), :] * probe_ref[g]
        zero = jnp.zeros_like(weighted)
        left = jnp.concatenate(
            [jnp.concatenate([weighted, zero], axis=1), jnp.concatenate([zero, weighted], axis=1)], axis=0
        ).astype(jnp.bfloat16)

        def route(j):
            t = place_ref[list_ref[g, j]]
            row = lax.shift_right_logical(t, 7)
            col = jnp.bitwise_and(t, 127)
            owner = lax.shift_right_logical(row, 5) * 32 + lax.shift_right_logical(col, 2)
            local = jnp.bitwise_and(col, 3) * DOWN + jnp.bitwise_and(row, 31)
            live = j < count
            owner = jnp.where(live, owner, 128)
            rank = jnp.minimum(seen_ref[owner], 1)
            seen_ref[owner] = rank + 1
            place = owner * 2 + rank
            table_ref[place] = local
            pos_ref[g * slots + j] = jnp.where(live, place, -1)
            return owner, rank

        def pair(j):
            both = jnp.dot(left, foot[g, 2 * j : 2 * j + 2].reshape(256, -1), preferred_element_type=jnp.float32)
            for u in range(2):
                owner, rank = route(2 * j + u)
                part = both[u * 8 : u * 8 + 8]
                part = jnp.concatenate([part[:, w * CELLS : (w + 1) * CELLS] for w in range(WEEKS)], axis=0)
                at = pl.multiple_of(rank * SLOT_ROWS, SLOT_ROWS)
                packed[owner, pl.ds(at, SLOT_ROWS), :] = part.astype(jnp.bfloat16)

        for n in range(3, pairs + 1):

            @pl.when((count + 1) // 2 == n)
            def _():
                for j in range(n):
                    fetch(g, j).wait()
                for j in range(n):
                    pair(j)
                for j in range(2 * n, slots):
                    pos_ref[g * slots + j] = -1

        return carry

    lax.fori_loop(0, groups, group, 0)

    first = lax.broadcasted_iota(jnp.int32, (8, CELLS), 0) < 4

    def note(d, carry):
        value = jnp.where(first, table_ref[2 * d], table_ref[2 * d + 1])
        packed[d, 64:72, :] = value.astype(jnp.float32).astype(jnp.bfloat16)
        return carry

    copies = []
    for k in range(4):
        lax.fori_loop(32 * k, 32 * k + 32, note, 0, unroll=8)
        part = pl.ds(32 * k, 32)
        copies.append(pltpu.make_async_copy(packed.at[part], out_hbm.at[part], out_sem.at[k]))
        copies[-1].start()
    for copy in copies:
        copy.wait()


def adjoint_call(tile_lists, counts, tile_place, probes, precision, footprints):
    groups, slots, sounds, span = footprints.shape
    smem = pl.BlockSpec(memory_space=pltpu.SMEM)
    hbm = pl.BlockSpec(memory_space=pltpu.HBM)
    return pl.pallas_call(
        adjoint_kernel,
        out_shape=(
            pltpu.HBM((128, SEND_ROWS, CELLS), jnp.bfloat16),
            jax.ShapeDtypeStruct((groups * slots,), jnp.int32),
        ),
        in_specs=[hbm] * 6,
        out_specs=(hbm, smem),
        scratch_shapes=[
            pltpu.VMEM((groups, slots, sounds, span), jnp.bfloat16),
            pltpu.VMEM((129, SEND_ROWS, CELLS), jnp.bfloat16),
            pltpu.VMEM(probes.shape, probes.dtype),
            pltpu.VMEM(precision.shape, precision.dtype),
            pltpu.SMEM(tile_lists.shape, jnp.int32),
            pltpu.SMEM(counts.shape, jnp.int32),
            pltpu.SMEM(tile_place.shape, jnp.int32),
            pltpu.SMEM((258,), jnp.int32),
            pltpu.SMEM((129,), jnp.int32),
            pltpu.SemaphoreType.DMA((5,)),
            pltpu.SemaphoreType.DMA((groups, slots // 2)),
            pltpu.SemaphoreType.DMA((4,)),
        ],
        compiler_params=pltpu.CompilerParams(vmem_limit_bytes=32 * MIB),
        name="adjoint",
    )(*map(in_hbm, (tile_lists, counts, tile_place, probes, precision, footprints)))


def receive_kernel(
    where_ref, arr_ref, scale_ref, hi_ref, lo_hbm, first_ref, second_ref, west_ref, east_ref, idx_ref,
    acc_a, acc_b, lo_ref, idx_vec, idx_sem, out_sem,
):
    zero = jnp.zeros((SLOT_ROWS, CELLS), jnp.float32)
    lane8 = lax.broadcasted_iota(jnp.int32, (8, CELLS), 1)

    def gather(d, found):
        return jnp.where(lane8 == d, arr_ref[d, 64:72, :].astype(jnp.float32), found)

    found = lax.fori_loop(0, 128, gather, jnp.zeros((8, CELLS), jnp.float32), unroll=8)
    idx_vec[...] = found.astype(jnp.int32)
    idx_copy = pltpu.make_async_copy(idx_vec, idx_ref, idx_sem)
    idx_copy.start()

    def clear(i, carry):
        acc_a[i] = zero
        acc_b[i] = zero
        return carry

    lax.fori_loop(0, TILES, clear, 0, unroll=8)
    idx_copy.wait()

    def add(d, carry):
        ia = idx_ref[0, d]
        ib = idx_ref[4, d]
        acc_a[ia] += arr_ref[d, :SLOT_ROWS, :].astype(jnp.float32)
        acc_b[ib] += arr_ref[d, SLOT_ROWS : 2 * SLOT_ROWS, :].astype(jnp.float32)
        return carry

    lax.fori_loop(0, 128, add, 0, unroll=4)

    lane = lax.broadcasted_iota(jnp.int32, (SLOT_ROWS, CELLS), 1)
    place = lax.shift_right_logical(jnp.bitwise_and(lane, 15), 2)

    copies = []
    even = jnp.bitwise_and(where_ref[0], 1) == 0
    for tc in (1, 2, 0, 3):

        def finish(quad, carry):
            edge = zero
            for k in range(4):
                tr = quad * 4 + k
                t = tc * DOWN + tr
                x = [acc_a[t, w * 8 : w * 8 + 8, :] + acc_b[t, w * 8 : w * 8 + 8, :] for w in range(WEEKS)]
                scale = scale_ref[tc, pl.ds(tr, 1), :]
                ahead = [x[0]]
                for w in range(1, WEEKS):
                    ahead.append(x[w] + week_decay * ahead[-1])
                mixed = [None] * WEEKS
                mixed[WEEKS - 1] = ahead[WEEKS - 1]
                behind = week_decay * x[WEEKS - 1]
                for w in range(WEEKS - 2, -1, -1):
                    mixed[w] = ahead[w] + behind
                    behind = week_decay * (x[w] + behind)
                y = jnp.concatenate(mixed, axis=0) * scale
                hi = y.astype(jnp.bfloat16)
                hi_ref[tc, tr] = hi
                lo_ref[tc, tr] = (y - hi.astype(jnp.float32)).astype(jnp.bfloat16)
                if tc == 0:
                    edge = jnp.where(place == k, pltpu.roll(y, 4 * k, 1), edge)
                if tc == ACROSS - 1:
                    edge = jnp.where(place == k, pltpu.roll(y, (4 * k - 12) % 128, 1), edge)
            if tc == 0:
                west_ref[quad] = edge.astype(jnp.bfloat16)
            if tc == ACROSS - 1:
                east_ref[quad] = edge.astype(jnp.bfloat16)
            return carry

        lax.fori_loop(0, QUADS, finish, 0)
        top = hi_ref[tc, 0]
        bottom = hi_ref[tc, DOWN - 1]
        first_ref[tc] = jnp.where(even, bottom, top)
        second_ref[tc] = jnp.where(even, top, bottom)
        copies.append(pltpu.make_async_copy(lo_ref.at[tc], lo_hbm.at[tc], out_sem.at[tc]))
        copies[-1].start()
    for copy in copies:
        copy.wait()


def receive_call(where, arrived, scale):
    vmem = pl.BlockSpec(memory_space=pltpu.VMEM)
    hbm = pl.BlockSpec(memory_space=pltpu.HBM)
    smem = pl.BlockSpec(memory_space=pltpu.SMEM)
    block = (ACROSS, DOWN, SLOT_ROWS, CELLS)
    row = jax.ShapeDtypeStruct((ACROSS, SLOT_ROWS, CELLS), jnp.bfloat16)
    column = jax.ShapeDtypeStruct((QUADS, SLOT_ROWS, CELLS), jnp.bfloat16)
    return pl.pallas_call(
        receive_kernel,
        out_shape=(
            jax.ShapeDtypeStruct(block, jnp.bfloat16),
            pltpu.HBM(block, jnp.bfloat16),
            row,
            row,
            column,
            column,
            jax.ShapeDtypeStruct((8, 128), jnp.int32),
        ),
        in_specs=[smem, vmem, vmem],
        out_specs=(vmem, hbm) + (vmem,) * 4 + (smem,),
        scratch_shapes=[
            pltpu.VMEM((TILES + 1, SLOT_ROWS, CELLS), jnp.float32),
            pltpu.VMEM((TILES + 1, SLOT_ROWS, CELLS), jnp.float32),
            pltpu.VMEM(block, jnp.bfloat16),
            pltpu.VMEM((8, 128), jnp.int32),
            pltpu.SemaphoreType.DMA,
            pltpu.SemaphoreType.DMA((ACROSS,)),
        ],
        compiler_params=pltpu.CompilerParams(vmem_limit_bytes=24 * MIB),
        name="receive",
    )(where, arrived, scale)


def facing(flag, first, second):
    even = jnp.bitwise_and(flag, 1) == 0
    return jnp.where(even, first, second), jnp.where(even, second, first)


def corner_kernel(where_ref, first_ref, second_ref, west_ref, east_ref, first_out, second_out):
    lane = lax.broadcasted_iota(jnp.int32, (SLOT_ROWS, CELLS), 1)
    place = lax.shift_right_logical(jnp.bitwise_and(lane, 15), 2)
    even = jnp.bitwise_and(where_ref[1], 1) == 0

    def put(quad, west, east):
        first_out[quad] = jnp.where(even, east, west)
        second_out[quad] = jnp.where(even, west, east)

    for quad in range(QUADS):
        put(quad, west_ref[quad], east_ref[quad])
    corners = []
    for tc, shift in ((0, 0), (ACROSS - 1, 116)):
        below, above = facing(
            where_ref[0], first_ref[tc].astype(jnp.float32), second_ref[tc].astype(jnp.float32)
        )
        if shift:
            above = pltpu.roll(above, shift, 1)
        below = pltpu.roll(below, (shift + 4) % 128, 1)
        corners.append(jnp.where(place == 0, above, below).astype(jnp.bfloat16))
    put(QUADS, *corners)


def corner_call(where, first, second, west, east):
    vmem = pl.BlockSpec(memory_space=pltpu.VMEM)
    column = jax.ShapeDtypeStruct((QUADS + 1, SLOT_ROWS, CELLS), jnp.bfloat16)
    return pl.pallas_call(
        corner_kernel,
        out_shape=(column, column),
        in_specs=[pl.BlockSpec(memory_space=pltpu.SMEM)] + [vmem] * 4,
        out_specs=(vmem, vmem),
        compiler_params=pltpu.CompilerParams(vmem_limit_bytes=16 * MIB),
        name="corner",
    )(where, first, second, west, east)


def diffuse_kernel(
    where_ref, idx_ref, hi_ref, lo_hbm, lat_first, lat_second, lon_first, lon_second, scale_ref, weight_hbm, mirror_hbm,
    inc_ref, reply_hbm,
    lo_ref, half_ref, nh, sh, wh, eh, left_ref, reply_ref, weight_ref, mirror_ref, reply_sem, const_sem, field_sem,
):
    lat, lon = where_ref[0], where_ref[1]
    flat = (SLOT_ROWS, CELLS)

    def mirrored(block, side):
        rows = block.reshape(-1, CELLS)
        out = jnp.dot(rows, mirror_ref[side], preferred_element_type=jnp.float32)
        return out.astype(jnp.bfloat16).reshape(block.shape)

    fields = [pltpu.make_async_copy(lo_hbm.at[tc], lo_ref.at[tc], field_sem.at[tc]) for tc in range(ACROSS)]
    for copy in fields:
        copy.start()
    mirror_copy = pltpu.make_async_copy(mirror_hbm, mirror_ref, const_sem.at[0])
    mirror_copy.start()
    weight_copy = pltpu.make_async_copy(weight_hbm, weight_ref, const_sem.at[1])
    weight_copy.start()
    for tc in range(ACROSS):
        sh[tc], nh[tc] = facing(lat, lat_first[tc], lat_second[tc])

    def unpack(i, quad, k):
        east, west = facing(lon, lon_first[quad].astype(jnp.float32), lon_second[quad].astype(jnp.float32))
        wh[i] = pltpu.roll(west, 12 - 4 * k, 1).astype(jnp.bfloat16)
        eh[i] = (pltpu.roll(east, 128 - 4 * k, 1) if k else east).astype(jnp.bfloat16)

    def unpack_quad(quad, carry):
        for k in range(4):
            unpack(quad * 4 + k + 1, quad, k)
        return carry

    lax.fori_loop(0, QUADS, unpack_quad, 0)
    unpack(0, QUADS, 0)
    unpack(DOWN + 1, QUADS, 1)
    mirror_copy.wait()

    @pl.when(lat == 0)
    def _():
        for tc in range(ACROSS):
            nh[tc] = mirrored(hi_ref[tc, 0], 0)

    @pl.when(lat == 3)
    def _():
        for tc in range(ACROSS):
            sh[tc] = mirrored(hi_ref[tc, DOWN - 1], 1)

    @pl.when(lon == 0)
    def _():
        wh[0] = mirrored(nh[0], 2)
        wh[1 : DOWN + 1] = mirrored(hi_ref[0], 2)
        wh[DOWN + 1] = mirrored(sh[0], 2)

    @pl.when(lon == 31)
    def _():
        eh[0] = mirrored(nh[ACROSS - 1], 3)
        eh[1 : DOWN + 1] = mirrored(hi_ref[ACROSS - 1], 3)
        eh[DOWN + 1] = mirrored(sh[ACROSS - 1], 3)

    @pl.when(lat == 0)
    def _():
        wh[0] = mirrored(wh[1], 0)
        eh[0] = mirrored(eh[1], 0)

    @pl.when(lat == 3)
    def _():
        wh[DOWN + 1] = mirrored(wh[DOWN], 1)
        eh[DOWN + 1] = mirrored(eh[DOWN], 1)

    lane = lax.broadcasted_iota(jnp.int32, flat, 1)
    upper = lane < 64
    east_side = jnp.bitwise_and(lane, 15) < 8
    chunk = 8
    zero = jnp.zeros(flat, jnp.bfloat16)
    weight_copy.wait()

    for pair in range(ACROSS // 2):
        for part in range(DOWN // chunk):
            total = None
            for ref, is_hi in ((hi_ref, True), (lo_ref, False)):
                if pair == 0 and part == 0 and not is_hi:
                    for copy in fields:
                        copy.wait()

                def tile(x, tr):
                    if x < 0 or x >= ACROSS:
                        if not is_hi:
                            return zero
                        return (wh if x < 0 else eh)[tr + 1]
                    if tr < 0 or tr >= DOWN:
                        if not is_hi:
                            return zero
                        return (nh if tr < 0 else sh)[x]
                    return ref[x, tr]

                for k in range(chunk):
                    tr = part * chunk + k
                    own, both = [], []
                    for x in range(2 * pair - 1, 2 * pair + 3):
                        own.append(tile(x, tr))
                        both.append(jnp.where(upper, tile(x, tr + 1), tile(x, tr - 1)))
                    rows = slice(k * SLOT_ROWS, (k + 1) * SLOT_ROWS)
                    left_ref[rows, 0:128] = own[1]
                    left_ref[rows, 128:256] = own[2]
                    left_ref[rows, 256:384] = jnp.where(east_side, own[3], own[0])
                    left_ref[rows, 384:512] = both[1]
                    left_ref[rows, 512:640] = both[2]
                    left_ref[rows, 640:768] = jnp.where(east_side, both[3], both[0])
                product = jnp.dot(left_ref[...], weight_ref[...], preferred_element_type=jnp.float32)
                total = product if total is None else total + product
            for k in range(chunk):
                tr = part * chunk + k
                for u in range(2):
                    tc = 2 * pair + u
                    scale = scale_ref[tc, tr : tr + 1, :] * STEP_FACTOR
                    y = total[k * SLOT_ROWS : (k + 1) * SLOT_ROWS, u * 128 : (u + 1) * 128] * scale
                    inc_ref[tc, tr] = y
                    half_ref[tc * DOWN + tr] = y.astype(jnp.bfloat16)

    def answer(d, carry):
        reply_ref[d, :SLOT_ROWS, :] = half_ref[idx_ref[0, d]]
        reply_ref[d, SLOT_ROWS:, :] = half_ref[idx_ref[4, d]]
        return carry

    copies = []
    for k in range(4):
        lax.fori_loop(32 * k, 32 * k + 32, answer, 0, unroll=8)
        part = pl.ds(32 * k, 32)
        copies.append(pltpu.make_async_copy(reply_ref.at[part], reply_hbm.at[part], reply_sem.at[k]))
        copies[-1].start()
    for copy in copies:
        copy.wait()


def diffuse_call(where, index, hi, lo, halos, scale, weight, mirror):
    vmem = pl.BlockSpec(memory_space=pltpu.VMEM)
    smem = pl.BlockSpec(memory_space=pltpu.SMEM)
    hbm = pl.BlockSpec(memory_space=pltpu.HBM)
    return pl.pallas_call(
        diffuse_kernel,
        out_shape=(
            jax.ShapeDtypeStruct((ACROSS, DOWN, SLOT_ROWS, CELLS), jnp.float32),
            pltpu.HBM((128, 2 * SLOT_ROWS, CELLS), jnp.bfloat16),
        ),
        in_specs=[smem, smem, vmem, hbm] + [vmem] * 5 + [hbm] * 2,
        out_specs=(vmem, hbm),
        scratch_shapes=[
            pltpu.VMEM((ACROSS, DOWN, SLOT_ROWS, CELLS), jnp.bfloat16),
            pltpu.VMEM((TILES + 1, SLOT_ROWS, CELLS), jnp.bfloat16),
            pltpu.VMEM((ACROSS, SLOT_ROWS, CELLS), jnp.bfloat16),
            pltpu.VMEM((ACROSS, SLOT_ROWS, CELLS), jnp.bfloat16),
            pltpu.VMEM((DOWN + 2, SLOT_ROWS, CELLS), jnp.bfloat16),
            pltpu.VMEM((DOWN + 2, SLOT_ROWS, CELLS), jnp.bfloat16),
            pltpu.VMEM((8 * SLOT_ROWS, 768), jnp.bfloat16),
            pltpu.VMEM((128, 2 * SLOT_ROWS, CELLS), jnp.bfloat16),
            pltpu.VMEM(weight.shape, weight.dtype),
            pltpu.VMEM(mirror.shape, mirror.dtype),
            pltpu.SemaphoreType.DMA((4,)),
            pltpu.SemaphoreType.DMA((2,)),
            pltpu.SemaphoreType.DMA((ACROSS,)),
        ],
        compiler_params=pltpu.CompilerParams(vmem_limit_bytes=32 * MIB),
        name="diffuse",
    )(where, index, hi, in_hbm(lo), *halos, scale, in_hbm(weight), in_hbm(mirror))


def layout_kernel(inc_ref, out_ref, rows_ref):
    lane = lax.broadcasted_iota(jnp.int32, (8, CELLS), 1)
    group = lax.shift_right_logical(lane, 4)

    def regroup(tr, carry):
        for half in range(2):
            v = [
                inc_ref[i % 4, tr, (half * 2 + i // 4) * 8 : (half * 2 + i // 4) * 8 + 8, :] for i in range(8)
            ]
            for bit in (1, 2, 4):
                clear = jnp.bitwise_and(group, bit) == 0
                for i in range(8):
                    if i & bit == 0:
                        a, c = v[i], v[i + bit]
                        v[i] = jnp.where(clear, a, pltpu.roll(c, 16 * bit, 1))
                        v[i + bit] = jnp.where(clear, pltpu.roll(a, 128 - 16 * bit, 1), c)
            for r in range(8):
                at = pl.multiple_of((half * 256 + tr * 8 + r) * 8, 8)
                rows_ref[pl.ds(at, 8), :] = v[r]
        return carry

    lax.fori_loop(0, DOWN, regroup, 0, unroll=2)

    for half in range(2):
        for p in range(PROBES):
            for k in range(2):
                block = rows_ref[pl.ds((half * 256 + k * 128) * 8 + p, 128, stride=8), :]
                out_ref[pl.ds((p * 4 + half * 2) * 64, 128), k * 128 : (k + 1) * 128] = block.T


def layout_call(inc):
    vmem = pl.BlockSpec(memory_space=pltpu.VMEM)
    return pl.pallas_call(
        layout_kernel,
        out_shape=jax.ShapeDtypeStruct((SLOT_ROWS * 64, 256), jnp.float32),
        in_specs=[vmem],
        out_specs=vmem,
        scratch_shapes=[pltpu.VMEM((2 * 256 * 8, CELLS), jnp.float32)],
        compiler_params=pltpu.CompilerParams(vmem_limit_bytes=16 * MIB),
        cost_estimate=pl.CostEstimate(flops=8 * MIB, bytes_accessed=8 * MIB, transcendentals=0),
        name="layout",
    )(inc)


def forward_kernel(pos_ref, tiles_ref, foot_hbm, out_ref, foot, foot_sem):
    groups, slots, sounds, span = foot.shape
    pairs = slots // 2

    def fetch(g, j):
        return pltpu.make_async_copy(foot_hbm.at[g, pl.ds(2 * j, 2)], foot.at[g, pl.ds(2 * j, 2)], foot_sem.at[g, j])

    def start_group(g, carry):
        for j in range(pairs):
            if j < 3:
                fetch(g, j).start()
            else:

                @pl.when(pos_ref[g * slots + 2 * j] >= 0)
                def _():
                    fetch(g, j).start()

        return carry

    lax.fori_loop(0, groups, start_group, 0)

    def group(g, carry):
        def one(j):
            found = pos_ref[g * slots + j]
            place = jnp.maximum(found, 0)
            at = pl.multiple_of(jnp.bitwise_and(place, 1) * SLOT_ROWS, SLOT_ROWS)
            tile = tiles_ref[lax.shift_right_logical(place, 1), pl.ds(at, SLOT_ROWS), :].astype(jnp.float32)
            left = jnp.concatenate([tile[w * 8 : w * 8 + 8] for w in range(WEEKS)], axis=1).astype(jnp.bfloat16)
            value = lax.dot_general(
                left, foot[g, j], (((1,), (1,)), ((), ())), preferred_element_type=jnp.float32
            )
            return value if j < 6 else jnp.where(found >= 0, value, 0.0)

        live = sum((pos_ref[g * slots + 2 * j] >= 0).astype(jnp.int32) for j in range(3, pairs)) + 3
        for n in range(3, pairs + 1):

            @pl.when(live == n)
            def _():
                for j in range(n):
                    fetch(g, j).wait()
                total = one(0)
                for j in range(1, 2 * n):
                    total = total + one(j)
                out_ref[g] = total

        return carry

    lax.fori_loop(0, groups, group, 0)


def forward_call(pos, tiles, footprints):
    groups, slots, sounds, span = footprints.shape
    smem = pl.BlockSpec(memory_space=pltpu.SMEM)
    vmem = pl.BlockSpec(memory_space=pltpu.VMEM)
    return pl.pallas_call(
        forward_kernel,
        out_shape=jax.ShapeDtypeStruct((groups, PROBES, sounds), jnp.float32),
        in_specs=[smem, vmem, pl.BlockSpec(memory_space=pltpu.HBM)],
        out_specs=vmem,
        scratch_shapes=[
            pltpu.VMEM(footprints.shape, footprints.dtype),
            pltpu.SemaphoreType.DMA((groups, slots // 2)),
        ],
        compiler_params=pltpu.CompilerParams(vmem_limit_bytes=32 * MIB),
        name="forward",
    )(pos, tiles, in_hbm(footprints))


def exchanged(block):
    return lax.all_to_all(block, ("lat", "lon"), split_axis=0, concat_axis=0, tiled=True)


def swaps(count, start):
    lower = [(i, i + 1) for i in range(start, count - 1, 2)]
    return lower + [(j, i) for i, j in lower]


def per_device(
    footprints, tile_lists, tile_counts, tile_place, probes, obs_precision, prior_sigma, land_mask
):
    lat, lon = lax.axis_index("lat"), lax.axis_index("lon")
    outgoing, pos = adjoint_call(tile_lists, tile_counts, tile_place, probes, obs_precision, footprints)
    arrived = exchanged(outgoing)

    scale = prior_sigma * land_mask.astype(jnp.float32)
    scale = scale.reshape(DOWN, TILE_ROWS, ACROSS, TILE_COLS).transpose(2, 0, 1, 3).reshape(ACROSS, DOWN, CELLS)

    where = jnp.stack([lat, lon]).astype(jnp.int32)
    hi, lo, lat_one, lat_two, left, right, index = receive_call(where, arrived, scale)
    lat_one = lax.ppermute(lat_one, "lat", swaps(4, 0))
    lat_two = lax.ppermute(lat_two, "lat", swaps(4, 1))
    lon_one, lon_two = corner_call(where, lat_one, lat_two, left, right)
    lon_one = lax.ppermute(lon_one, "lon", swaps(32, 0))
    lon_two = lax.ppermute(lon_two, "lon", swaps(32, 1))
    halos = (lat_one, lat_two, lon_one, lon_two)

    weight = jnp.asarray(stencil_weights(), jnp.bfloat16)
    mirror = jnp.asarray(reflections(), jnp.bfloat16)
    inc, reply = diffuse_call(where, index, hi, lo, halos, scale, weight, mirror)
    returned = exchanged(reply)
    increment = layout_call(inc).reshape(SLOT_ROWS, 64, 256).transpose(2, 0, 1)
    predicted = forward_call(pos, returned, footprints)
    return (predicted, increment)


def solution(mesh):
    in_specs = (
        P(("lat", "lon"), None, None, None),
        P(("lat", "lon"), None),
        P(("lat", "lon")),
        P(),
        P(("lat", "lon"), None, None),
        P(("lat", "lon"), None),
        P("lat", "lon"),
        P("lat", "lon"),
    )
    out_specs = (P(("lat", "lon"), None, None), P("lat", None, "lon"))
    return jax.shard_map(
        per_device, mesh=mesh, in_specs=in_specs, out_specs=out_specs, check_vma=False
    )
```

time: 170 us -> 126 us (0.74)
  blocking collectives: 52.4 us -> 0 us
  waiting for transfers between devices: 26.6 us -> 58.5 us
  local copies, waits for them, and re-layouts: 23.9 us -> 3.72 us
  starting transfers between devices: 35.8 us -> 26.3 us
  Pallas kernels: 29.2 us -> 35.9 us
    all_gather x1 -> x0, blocking collectives: 52.4 us -> none  [per_device(): tables = lax.all_gather(table, ('lat', 'lon'), axis=0, tiled=False)]
    all_to_all x2, waiting for transfers between devices: 23 us -> 55.3 us  [exchanged(): lax.all_to_all(block, ('lat', 'lon'), split_axis=0, concat_axis=0, tiled=...]
    unnamed x30 -> x8, local copies, waits for them, and re-layouts: 20.5 us -> 2.91 us
    ppermute x4, starting transfers between devices: 8.44 us -> 2.11 us  [the longest x1 0.72 us: per_device(): lat_one = lax.ppermute(lat_one, 'lat', swaps(4, 0))]
    pallas_call x2 -> x3, Pallas kernels: 10.9 us -> 14.8 us  [the longest x1 8.78 us: adjoint_call(): pl.pallas_call(adjoint_kernel, out_shape=(pltpu.HBM((128, SEND_ROWS, CELL...]
    all_to_all x2, starting transfers between devices: 27.4 us -> 24.2 us  [exchanged(): lax.all_to_all(block, ('lat', 'lon'), split_axis=0, concat_axis=0, tiled=...]
    pallas_call x1, Pallas kernels: 4.56 us -> 6.97 us  [diffuse_call(): pl.pallas_call(diffuse_kernel, out_shape=(jax.ShapeDtypeStruct((ACROSS, D...]
  transfers between devices with their start and end apart: 6 -> 6, of which waited for: 3 -> 4; matrix products, arithmetic and copies ran while one was open for 1% -> 1% of each run, Pallas kernels for 3% -> 5%
where the time goes in v1:
time: 126 us; the launch traced here: 125 us
  waiting for transfers between devices  58.5 us (46%)
  Pallas kernels  35.9 us (28%)
  starting transfers between devices  26.3 us (21%)
  local copies, waits for them, and re-layouts  3.72 us (3%)
    all_to_all x2, waiting for transfers between devices, exchanged(): lax.all_to_all(block, ('lat', 'lon'), split_axis=0, concat_axis=0, tiled=...  55.3 us
    all_to_all x2, starting transfers between devices, exchanged(): lax.all_to_all(block, ('lat', 'lon'), split_axis=0, concat_axis=0, tiled=...  24.2 us
    pallas_call x1, Pallas kernels, adjoint_call(): pl.pallas_call(adjoint_kernel, out_shape=(pltpu.HBM((128, SEND_ROWS, CELL...  8.78 us
    pallas_call x1, Pallas kernels, forward_call(): pl.pallas_call(forward_kernel, out_shape=jax.ShapeDtypeStruct((groups, PR...  8.35 us
    pallas_call x1, Pallas kernels, diffuse_call(): pl.pallas_call(diffuse_kernel, out_shape=(jax.ShapeDtypeStruct((ACROSS, D...  6.97 us
    pallas_call x1, Pallas kernels, layout_call(): pl.pallas_call(layout_kernel, out_shape=jax.ShapeDtypeStruct((SLOT_ROWS *...  5.83 us
    pallas_call x1, Pallas kernels, receive_call(): pl.pallas_call(receive_kernel, out_shape=(jax.ShapeDtypeStruct(block, jnp...  5.36 us
    unnamed x8, local copies, waits for them, and re-layouts  2.91 us
  transfers between devices with their start and end apart: 6, of which 4 were waited for; matrix products, arithmetic and copies ran while one was open for 1% of the time, Pallas kernels for 5%

profile of v1, /device:TPU:0, one launch (start us, length us, event | category | flops | bytes accessed | tf_op | source)
XLA Modules:
  0.0 125.3 jit_solution(9919760312058101663)
XLA Ops:
  0.6 8.8 %adjoint.1 = (bf16[128,72,128]{2,1,0:T(8,128)(2,1)}, s32[144]{0:T(256)S(1)}) custom-call(s32[12,12]{1,0:T(8,128)} %list_hbm.1, s32[12]{0:T(128)} %count_hbm.1, s32[16384]{0:T(1024)} %place_hbm.1, f32[12,8,128]{2,1,0:T(8,128)} %probe_hbm.1, f32[12,128]{1,0:T(8,128)} %prec_hbm.1, bf16[12,12,128,512]{3,2,1,0:T(8,128)(2,1)} %foot_hbm.3), custom_call_target="tpu_custom_call" | custom-call | tf_op jit(solution)/shard_map/adjoint/pallas_call | solution.py:206
  9.4 0.0 copy-start.2
  9.4 0.0 copy-start.3
  9.4 11.4 %all-to-all-start = ((bf16[128,72,128]{2,1,0:T(8,128)(2,1)}), bf16[128,72,128]{2,1,0:T(8,128)(2,1)S(1)}, u32[]{:S(2)}, u32[]{:S(2)}) async-start(bf16[128,72,128]{2,1,0:T(8,128)(2,1)} %get-tuple-element.16), calls=%async_computation | async-start | bytes 4718592 | tf_op jit(solution)/shard_map/all_to_all | solution.py:667
  20.8 0.0 copy-done.2
  20.8 0.0 copy-done.3
  20.9 0.1 copy.13
  21.0 0.3 reshape.13
  21.2 0.3 copy.14
  21.6 0.1 copy.15.scale_ref
  21.7 0.1 pad_add_fusion.where_ref
  21.8 32.3 %all-to-all-done.arr_ref = bf16[128,72,128]{2,1,0:T(8,128)(2,1)S(1)} async-done(((bf16[128,72,128]{2,1,0:T(8,128)(2,1)}), bf16[128,72,128]{2,1,0:T(8,128)(2,1)S(1)}, u32[]{:S(2)}, u32[]{:S(2)}) %all-to-all-start) | async-done | bytes 2359328 | tf_op jit(solution)/shard_map/all_to_all | solution.py:667
  54.0 5.4 %receive.1 = (bf16[4,32,32,128]{3,2,1,0:T(8,128)(2,1)S(1)}, bf16[4,32,32,128]{3,2,1,0:T(8,128)(2,1)}, bf16[4,32,128]{2,1,0:T(8,128)(2,1)S(1)}, bf16[4,32,128]{2,...) custom-call(s32[2]{0:T(128)S(1)} %pad_add_fusion.where_ref, ...), custom_call_target="tpu_custom_call" | custom-call | tf_op jit(solution)/shard_map/receive/pallas_call | solution.py:320
  59.4 0.7 collective-permute-start
  60.1 0.7 collective-permute-start.1
  60.8 2.6 %collective-permute-done.first_ref.lat_first = bf16[4,32,128]{2,1,0:T(8,128)(2,1)S(1)} collective-permute-done((bf16[4,32,128]{2,1,0:T(8,128)(2,1)S(1)}, bf16[4,32,128]{2,1,0:T(8,128)(2,1)S(1)}, u32[]{:S(2)}, u32[]{:S(2)}) %collective-permute-start) | collective-permute-done | bytes 32800 | tf_op jit(solution)/shard_map/ppermute | solution.py:687
  63.4 0.0 collective-permute-done.1.second_ref.lat_second
  63.4 0.6 corner.1
  64.0 0.1 collective-permute-start.2
  64.1 0.7 collective-permute-start.3
  64.8 0.6 collective-permute-done.2.lon_first
  65.4 0.0 collective-permute-done.3.lon_second
  65.4 7.0 %diffuse.1 = (f32[4,32,32,128]{3,2,1,0:T(8,128)S(1)}, bf16[128,64,128]{2,1,0:T(8,128)(2,1)}) custom-call(s32[2]{0:T(128)S(1)} %pad_add_fusion.where_ref, s32[8,128]{1,0:T(8,128)S(1)} %get-tuple-element.17.idx_ref, bf16[4,32,32,128]{3,2,1,0:T(8,128)(2,1)S(1)} %get-tuple-element.18.hi_ref, bf16[4,32,32,128]{3,2,1,0:T(8,128)(2,1)} %get-tuple-element.19.lo_hbm, ...), custom_call_target="tpu_custom_call" | custom-call | tf_op jit(solution)/shard_map/diffuse/pallas_call | solution.py:526
  72.4 0.0 copy-start
  72.4 1.3 %copy-done = f32[4,32,32,128]{3,2,1,0:T(8,128)} copy-done((f32[4,32,32,128]{3,2,1,0:T(8,128)}, f32[4,32,32,128]{3,2,1,0:T(8,128)S(1)}, u32[]{:S(2)}) %copy-start) | copy-done | bytes 2097176
  73.7 12.8 %all-to-all-start.1 = ((bf16[128,64,128]{2,1,0:T(8,128)(2,1)}), bf16[128,64,128]{2,1,0:T(8,128)(2,1)S(1)}, u32[]{:S(2)}, u32[]{:S(2)}) async-start(bf16[128,64,128]{2,1,0:T(8,128)(2,1)} %get-tuple-element.26), calls=%async_computation.1 | async-start | bytes 4194304 | tf_op jit(solution)/shard_map/all_to_all | solution.py:667
  86.5 0.0 copy-start.1
  86.5 1.6 %copy-done.1 = f32[4,32,32,128]{3,2,1,0:T(8,128)S(1)} copy-done((f32[4,32,32,128]{3,2,1,0:T(8,128)S(1)}, f32[4,32,32,128]{3,2,1,0:T(8,128)}, u32[]{:S(2)}) %copy-start.1) | copy-done | bytes 2097176
  88.1 5.8 %layout.1 = f32[2048,256]{1,0:T(8,128)} custom-call(f32[4,32,32,128]{3,2,1,0:T(8,128)S(1)} %copy-done.1), custom_call_target="tpu_custom_call" | custom-call | flops 8388608 | bytes 8388608 | tf_op jit(solution)/shard_map/layout/pallas_call | solution.py:586
  94.0 23.0 %all-to-all-done.1.tiles_ref = bf16[128,64,128]{2,1,0:T(8,128)(2,1)S(1)} async-done(((bf16[128,64,128]{2,1,0:T(8,128)(2,1)}), bf16[128,64,128]{2,1,0:T(8,128)(2,1)S(1)}, u32[]{:S(2)}, u32[]{:S(2)}) %all-to-all-start.1) | async-done | bytes 2097184 | tf_op jit(solution)/shard_map/all_to_all | solution.py:667
  117.0 8.4 %forward.1 = f32[12,8,128]{2,1,0:T(8,128)} custom-call(s32[144]{0:T(256)S(1)} %get-tuple-element.15.pos_ref, bf16[128,64,128]{2,1,0:T(8,128)(2,1)S(1)} %all-to-all-done.1.tiles_ref, bf16[12,12,128,512]{3,2,1,0:T(8,128)(2,1)} %foot_hbm.3), custom_call_target="tpu_custom_call" | custom-call | tf_op jit(solution)/shard_map/forward/pallas_call | solution.py:652
  (1 shorter events, 0.0 us)
Async XLA Ops:
  9.4 11.4 %copy-start.2 = (f32[256,64]{0,1:T(8,128)S(1)}, f32[256,64]{0,1:T(8,128)}, u32[]{:S(2)}) copy-start(f32[256,64]{0,1:T(8,128)} %param.16) | copy-start | bytes 196612
  9.4 11.4 %copy-start.3 = (s32[256,64]{0,1:T(8,128)S(1)}, s32[256,64]{0,1:T(8,128)}, u32[]{:S(2)}) copy-start(s32[256,64]{0,1:T(8,128)} %param.17) | copy-start | bytes 196612
  9.4 44.6 %all-to-all-start = ((bf16[128,72,128]{2,1,0:T(8,128)(2,1)}), bf16[128,72,128]{2,1,0:T(8,128)(2,1)S(1)}, u32[]{:S(2)}, u32[]{:S(2)}) async-start(bf16[128,72,128]{2,1,0:T(8,128)(2,1)} %get-tuple-element.16), calls=%async_computation | async-start | bytes 4718592 | tf_op jit(solution)/shard_map/all_to_all | solution.py:667
  59.4 4.0 %collective-permute-start = (bf16[4,32,128]{2,1,0:T(8,128)(2,1)S(1)}, bf16[4,32,128]{2,1,0:T(8,128)(2,1)S(1)}, u32[]{:S(2)}, u32[]{:S(2)}) collective-permute-start(bf16[4,32,128]{2,1,0:T(8,128)(2,1)S(1)} %get-tuple-element.20), channel_id=1, source_target_pairs={{0,32},{64,96},{32,0},{96,64},{1,33},{65,97},{33,1},{97,65},{2,34}... | collective-permute-start | bytes 98312 | tf_op jit(solution)/shard_map/ppermute | solution.py:687
  60.1 3.3 %collective-permute-start.1 = (bf16[4,32,128]{2,1,0:T(8,128)(2,1)S(1)}, bf16[4,32,128]{2,1,0:T(8,128)(2,1)S(1)}, u32[]{:S(2)}, u32[]{:S(2)}) collective-permute-start(bf16[4,32,128]{2,1,0:T(8,128)(2,1)S(1)} %get-tuple-element.21), channel_id=1, source_target_pairs={{32,64},{64,32},{33,65},{65,33},{34,66},{66,34},{35,67},{67,35},{3... | collective-permute-start | bytes 98312 | tf_op jit(solution)/shard_map/ppermute | solution.py:688
  64.0 1.3 %collective-permute-start.2 = (bf16[9,32,128]{2,1,0:T(8,128)(2,1)S(1)}, bf16[9,32,128]{2,1,0:T(8,128)(2,1)S(1)}, u32[]{:S(2)}, u32[]{:S(2)}) collective-permute-start(bf16[9,32,128]{2,1,0:T(8,128)(2,1)S(1)} %get-tuple-element.24), channel_id=1, source_target_pairs={{0,1},{2,3},{4,5},{6,7},{8,9},{10,11},{12,13},{14,15},{16,17},{18,... | collective-permute-start | bytes 221192 | tf_op jit(solution)/shard_map/ppermute | solution.py:690
  64.1 1.3 %collective-permute-start.3 = (bf16[9,32,128]{2,1,0:T(8,128)(2,1)S(1)}, bf16[9,32,128]{2,1,0:T(8,128)(2,1)S(1)}, u32[]{:S(2)}, u32[]{:S(2)}) collective-permute-start(bf16[9,32,128]{2,1,0:T(8,128)(2,1)S(1)} %get-tuple-element.25), channel_id=1, source_target_pairs={{1,2},{3,4},{5,6},{7,8},{9,10},{11,12},{13,14},{15,16},{17,18},{19... | collective-permute-start | bytes 221192 | tf_op jit(solution)/shard_map/ppermute | solution.py:691
  72.4 1.3 %copy-start = (f32[4,32,32,128]{3,2,1,0:T(8,128)}, f32[4,32,32,128]{3,2,1,0:T(8,128)S(1)}, u32[]{:S(2)}) copy-start(f32[4,32,32,128]{3,2,1,0:T(8,128)S(1)} %get-tuple-element.27.inc_ref) | copy-start | bytes 6291460
  73.7 43.3 %all-to-all-start.1 = ((bf16[128,64,128]{2,1,0:T(8,128)(2,1)}), bf16[128,64,128]{2,1,0:T(8,128)(2,1)S(1)}, u32[]{:S(2)}, u32[]{:S(2)}) async-start(bf16[128,64,128]{2,1,0:T(8,128)(2,1)} %get-tuple-element.26), calls=%async_computation.1 | async-start | bytes 4194304 | tf_op jit(solution)/shard_map/all_to_all | solution.py:667
  86.5 1.6 %copy-start.1 = (f32[4,32,32,128]{3,2,1,0:T(8,128)S(1)}, f32[4,32,32,128]{3,2,1,0:T(8,128)}, u32[]{:S(2)}) copy-start(f32[4,32,32,128]{3,2,1,0:T(8,128)} %copy-done) | copy-start | bytes 6291460

commit v2 on v1

--- a/solution.py
+++ b/solution.py
@@ -20,6 +20,8 @@
 TILES = DOWN * ACROSS
 SEND_ROWS = 2 * SLOT_ROWS + 8
 QUADS = DOWN // 4
+DIFFUSE_CHUNK = 8
+LEAST = 6
 
 diffusion_rate = 0.2
 week_decay = 0.6
@@ -78,10 +80,10 @@
 
 def adjoint_kernel(
     list_hbm, count_hbm, place_hbm, probe_hbm, prec_hbm, foot_hbm, out_hbm, pos_ref,
-    foot, packed, probe_ref, prec_ref, list_ref, count_ref, place_ref, table_ref, seen_ref, small_sem, foot_sem, out_sem,
+    foot, packed, probe_ref, prec_ref, list_ref, count_ref, place_ref, seen_ref, small_sem, foot_sem, out_sem,
 ):
     groups, slots = foot.shape[:2]
-    pairs = slots // 2
+
     small = [
         pltpu.make_async_copy(src, dst, small_sem.at[k])
         for k, (src, dst) in enumerate(
@@ -97,21 +99,21 @@
     for copy in small:
         copy.start()
 
-    def fetch(g, j):
-        return pltpu.make_async_copy(foot_hbm.at[g, pl.ds(2 * j, 2)], foot.at[g, pl.ds(2 * j, 2)], foot_sem.at[g, j])
+    def fetch(g, first, last):
+        part = (g, pl.ds(first, last - first))
+        return pltpu.make_async_copy(foot_hbm.at[part], foot.at[part], foot_sem.at[g, first // LEAST])
 
     def start_sure(g, carry):
-        for j in range(3):
-            fetch(g, j).start()
+        fetch(g, 0, LEAST).start()
         return carry
 
     def start_rest(g, carry):
         count = count_ref[g]
-        for j in range(3, pairs):
-
-            @pl.when(2 * j < count)
+        for n in range(LEAST + 1, slots + 1):
+
+            @pl.when(count == n)
             def _():
-                fetch(g, j).start()
+                fetch(g, LEAST, n).start()
 
         return carry
 
@@ -125,23 +127,21 @@
 
     lax.fori_loop(1, groups, start_group, 0)
 
+    nobody = jnp.full((8, CELLS), TILES, jnp.float32).astype(jnp.bfloat16)
+    number_row = lax.shift_right_logical(lax.broadcasted_iota(jnp.int32, (8, CELLS), 0), 2)
+
     def clear(i, carry):
-        table_ref[2 * i] = TILES
-        table_ref[2 * i + 1] = TILES
         seen_ref[i] = 0
-        return carry
-
-    lax.fori_loop(0, 129, clear, 0, unroll=3)
+        packed[i, 2 * SLOT_ROWS :, :] = nobody
+        return carry
+
+    lax.fori_loop(0, 128, clear, 0, unroll=8)
     for copy in small[1:]:
         copy.wait()
 
     def group(g, carry):
         count = count_ref[g]
-        weighted = prec_ref[pl.ds(g, 1), :] * probe_ref[g]
-        zero = jnp.zeros_like(weighted)
-        left = jnp.concatenate(
-            [jnp.concatenate([weighted, zero], axis=1), jnp.concatenate([zero, weighted], axis=1)], axis=0
-        ).astype(jnp.bfloat16)
+        weighted = (prec_ref[pl.ds(g, 1), :] * probe_ref[g]).astype(jnp.bfloat16)
 
         def route(j):
             t = place_ref[list_ref[g, j]]
@@ -149,49 +149,40 @@
             col = jnp.bitwise_and(t, 127)
             owner = lax.shift_right_logical(row, 5) * 32 + lax.shift_right_logical(col, 2)
             local = jnp.bitwise_and(col, 3) * DOWN + jnp.bitwise_and(row, 31)
-            live = j < count
-            owner = jnp.where(live, owner, 128)
             rank = jnp.minimum(seen_ref[owner], 1)
             seen_ref[owner] = rank + 1
-            place = owner * 2 + rank
-            table_ref[place] = local
-            pos_ref[g * slots + j] = jnp.where(live, place, -1)
-            return owner, rank
-
-        def pair(j):
-            both = jnp.dot(left, foot[g, 2 * j : 2 * j + 2].reshape(256, -1), preferred_element_type=jnp.float32)
-            for u in range(2):
-                owner, rank = route(2 * j + u)
-                part = both[u * 8 : u * 8 + 8]
-                part = jnp.concatenate([part[:, w * CELLS : (w + 1) * CELLS] for w in range(WEEKS)], axis=0)
-                at = pl.multiple_of(rank * SLOT_ROWS, SLOT_ROWS)
-                packed[owner, pl.ds(at, SLOT_ROWS), :] = part.astype(jnp.bfloat16)
-
-        for n in range(3, pairs + 1):
-
-            @pl.when((count + 1) // 2 == n)
+            pos_ref[g * slots + j] = owner * 2 + rank
+            return owner, rank, local
+
+        def slot(j):
+            part = jnp.dot(weighted, foot[g, j], preferred_element_type=jnp.float32)
+            owner, rank, local = route(j)
+            part = jnp.concatenate([part[:, w * CELLS : (w + 1) * CELLS] for w in range(WEEKS)], axis=0)
+            at = pl.multiple_of(rank * SLOT_ROWS, SLOT_ROWS)
+            packed[owner, pl.ds(at, SLOT_ROWS), :] = part.astype(jnp.bfloat16)
+            numbers = packed[owner, 2 * SLOT_ROWS :, :].astype(jnp.float32)
+            numbers = jnp.where(number_row == rank, local.astype(jnp.float32), numbers)
+            packed[owner, 2 * SLOT_ROWS :, :] = numbers.astype(jnp.bfloat16)
+
+        for n in range(LEAST, slots + 1):
+
+            @pl.when(count == n)
             def _():
+                fetch(g, 0, LEAST).wait()
+                if n > LEAST:
+                    fetch(g, LEAST, n).wait()
                 for j in range(n):
-                    fetch(g, j).wait()
-                for j in range(n):
-                    pair(j)
-                for j in range(2 * n, slots):
-                    pos_ref[g * slots + j] = -1
+                    slot(j)
+                for j in range(n, slots):
+                    pos_ref[g * slots + j] = 0
+                pos_ref[groups * slots + g] = n
 
         return carry
 
     lax.fori_loop(0, groups, group, 0)
-
-    first = lax.broadcasted_iota(jnp.int32, (8, CELLS), 0) < 4
-
-    def note(d, carry):
-        value = jnp.where(first, table_ref[2 * d], table_ref[2 * d + 1])
-        packed[d, 64:72, :] = value.astype(jnp.float32).astype(jnp.bfloat16)
-        return carry
 
     copies = []
     for k in range(4):
-        lax.fori_loop(32 * k, 32 * k + 32, note, 0, unroll=8)
         part = pl.ds(32 * k, 32)
         copies.append(pltpu.make_async_copy(packed.at[part], out_hbm.at[part], out_sem.at[k]))
         copies[-1].start()
@@ -207,22 +198,21 @@
         adjoint_kernel,
         out_shape=(
             pltpu.HBM((128, SEND_ROWS, CELLS), jnp.bfloat16),
-            jax.ShapeDtypeStruct((groups * slots,), jnp.int32),
+            jax.ShapeDtypeStruct((groups * slots + groups,), jnp.int32),
         ),
         in_specs=[hbm] * 6,
         out_specs=(hbm, smem),
         scratch_shapes=[
             pltpu.VMEM((groups, slots, sounds, span), jnp.bfloat16),
-            pltpu.VMEM((129, SEND_ROWS, CELLS), jnp.bfloat16),
+            pltpu.VMEM((128, SEND_ROWS, CELLS), jnp.bfloat16),
             pltpu.VMEM(probes.shape, probes.dtype),
             pltpu.VMEM(precision.shape, precision.dtype),
             pltpu.SMEM(tile_lists.shape, jnp.int32),
             pltpu.SMEM(counts.shape, jnp.int32),
             pltpu.SMEM(tile_place.shape, jnp.int32),
-            pltpu.SMEM((258,), jnp.int32),
-            pltpu.SMEM((129,), jnp.int32),
+            pltpu.SMEM((128,), jnp.int32),
             pltpu.SemaphoreType.DMA((5,)),
-            pltpu.SemaphoreType.DMA((groups, slots // 2)),
+            pltpu.SemaphoreType.DMA((groups, 2)),
             pltpu.SemaphoreType.DMA((4,)),
         ],
         compiler_params=pltpu.CompilerParams(vmem_limit_bytes=32 * MIB),
@@ -231,8 +221,8 @@
 
 
 def receive_kernel(
-    where_ref, arr_ref, scale_ref, hi_ref, lo_hbm, first_ref, second_ref, west_ref, east_ref, idx_ref,
-    acc_a, acc_b, lo_ref, idx_vec, idx_sem, out_sem,
+    where_ref, arr_ref, scale_ref, hi_hbm, lo_hbm, first_ref, second_ref, west_ref, east_ref, idx_ref,
+    acc_a, acc_b, hi_ref, lo_ref, idx_vec, idx_sem, out_sem,
 ):
     zero = jnp.zeros((SLOT_ROWS, CELLS), jnp.float32)
     lane8 = lax.broadcasted_iota(jnp.int32, (8, CELLS), 1)
@@ -240,7 +230,7 @@
     def gather(d, found):
         return jnp.where(lane8 == d, arr_ref[d, 64:72, :].astype(jnp.float32), found)
 
-    found = lax.fori_loop(0, 128, gather, jnp.zeros((8, CELLS), jnp.float32), unroll=8)
+    found = lax.fori_loop(0, 128, gather, jnp.zeros((8, CELLS), jnp.float32), unroll=16)
     idx_vec[...] = found.astype(jnp.int32)
     idx_copy = pltpu.make_async_copy(idx_vec, idx_ref, idx_sem)
     idx_copy.start()
@@ -260,7 +250,7 @@
         acc_b[ib] += arr_ref[d, SLOT_ROWS : 2 * SLOT_ROWS, :].astype(jnp.float32)
         return carry
 
-    lax.fori_loop(0, 128, add, 0, unroll=4)
+    lax.fori_loop(0, 128, add, 0, unroll=8)
 
     lane = lax.broadcasted_iota(jnp.int32, (SLOT_ROWS, CELLS), 1)
     place = lax.shift_right_logical(jnp.bitwise_and(lane, 15), 2)
@@ -299,12 +289,14 @@
                 east_ref[quad] = edge.astype(jnp.bfloat16)
             return carry
 
-        lax.fori_loop(0, QUADS, finish, 0)
+        lax.fori_loop(0, QUADS, finish, 0, unroll=2)
         top = hi_ref[tc, 0]
         bottom = hi_ref[tc, DOWN - 1]
         first_ref[tc] = jnp.where(even, bottom, top)
         second_ref[tc] = jnp.where(even, top, bottom)
-        copies.append(pltpu.make_async_copy(lo_ref.at[tc], lo_hbm.at[tc], out_sem.at[tc]))
+        copies.append(pltpu.make_async_copy(hi_ref.at[tc], hi_hbm.at[tc], out_sem.at[0, tc]))
+        copies.append(pltpu.make_async_copy(lo_ref.at[tc], lo_hbm.at[tc], out_sem.at[1, tc]))
+        copies[-2].start()
         copies[-1].start()
     for copy in copies:
         copy.wait()
@@ -320,7 +312,7 @@
     return pl.pallas_call(
         receive_kernel,
         out_shape=(
-            jax.ShapeDtypeStruct(block, jnp.bfloat16),
+            pltpu.HBM(block, jnp.bfloat16),
             pltpu.HBM(block, jnp.bfloat16),
             row,
             row,
@@ -329,14 +321,15 @@
             jax.ShapeDtypeStruct((8, 128), jnp.int32),
         ),
         in_specs=[smem, vmem, vmem],
-        out_specs=(vmem, hbm) + (vmem,) * 4 + (smem,),
+        out_specs=(hbm, hbm) + (vmem,) * 4 + (smem,),
         scratch_shapes=[
             pltpu.VMEM((TILES + 1, SLOT_ROWS, CELLS), jnp.float32),
             pltpu.VMEM((TILES + 1, SLOT_ROWS, CELLS), jnp.float32),
             pltpu.VMEM(block, jnp.bfloat16),
+            pltpu.VMEM(block, jnp.bfloat16),
             pltpu.VMEM((8, 128), jnp.int32),
             pltpu.SemaphoreType.DMA,
-            pltpu.SemaphoreType.DMA((ACROSS,)),
+            pltpu.SemaphoreType.DMA((2, ACROSS)),
         ],
         compiler_params=pltpu.CompilerParams(vmem_limit_bytes=24 * MIB),
         name="receive",
@@ -385,116 +378,118 @@
 
 
 def diffuse_kernel(
-    where_ref, idx_ref, hi_ref, lo_hbm, lat_first, lat_second, lon_first, lon_second, scale_ref, weight_hbm, mirror_hbm,
-    inc_ref, reply_hbm,
-    lo_ref, half_ref, nh, sh, wh, eh, left_ref, reply_ref, weight_ref, mirror_ref, reply_sem, const_sem, field_sem,
+    where_ref, idx_ref, hi_hbm, lo_hbm, lat_first, lat_second, lon_first, lon_second,
+    scale_ref, weight_hbm, mirror_hbm,
+    inc_hbm, reply_hbm,
+    hi_ref, lo_ref, inc_ref, half_ref, reply_ref, weight_ref, mirror_ref,
+    reply_sem, const_sem, field_sem, inc_sem,
 ):
     lat, lon = where_ref[0], where_ref[1]
-    flat = (SLOT_ROWS, CELLS)
+    last_row, last_col = DOWN + 1, ACROSS + 1
 
     def mirrored(block, side):
         rows = block.reshape(-1, CELLS)
         out = jnp.dot(rows, mirror_ref[side], preferred_element_type=jnp.float32)
         return out.astype(jnp.bfloat16).reshape(block.shape)
 
-    fields = [pltpu.make_async_copy(lo_hbm.at[tc], lo_ref.at[tc], field_sem.at[tc]) for tc in range(ACROSS)]
+    fields = []
+    for tc in range(ACROSS):
+        fields.append(pltpu.make_async_copy(hi_hbm.at[tc], hi_ref.at[tc + 1, pl.ds(1, DOWN)], field_sem.at[0, tc]))
+    for tc in range(ACROSS):
+        fields.append(pltpu.make_async_copy(lo_hbm.at[tc], lo_ref.at[tc], field_sem.at[1, tc]))
     for copy in fields:
         copy.start()
     mirror_copy = pltpu.make_async_copy(mirror_hbm, mirror_ref, const_sem.at[0])
     mirror_copy.start()
     weight_copy = pltpu.make_async_copy(weight_hbm, weight_ref, const_sem.at[1])
     weight_copy.start()
-    for tc in range(ACROSS):
-        sh[tc], nh[tc] = facing(lat, lat_first[tc], lat_second[tc])
-
-    def unpack(i, quad, k):
-        east, west = facing(lon, lon_first[quad].astype(jnp.float32), lon_second[quad].astype(jnp.float32))
-        wh[i] = pltpu.roll(west, 12 - 4 * k, 1).astype(jnp.bfloat16)
-        eh[i] = (pltpu.roll(east, 128 - 4 * k, 1) if k else east).astype(jnp.bfloat16)
+
+    def unpack(i, one, two, k):
+        east, west = facing(lon, one.astype(jnp.float32), two.astype(jnp.float32))
+        hi_ref[0, i] = pltpu.roll(west, 12 - 4 * k, 1).astype(jnp.bfloat16)
+        hi_ref[last_col, i] = (pltpu.roll(east, 128 - 4 * k, 1) if k else east).astype(jnp.bfloat16)
 
     def unpack_quad(quad, carry):
         for k in range(4):
-            unpack(quad * 4 + k + 1, quad, k)
-        return carry
-
-    lax.fori_loop(0, QUADS, unpack_quad, 0)
-    unpack(0, QUADS, 0)
-    unpack(DOWN + 1, QUADS, 1)
+            i = quad * 4 + k + 1
+            unpack(i, lon_first[quad], lon_second[quad], k)
+        return carry
+
+    lax.fori_loop(0, QUADS, unpack_quad, 0, unroll=2)
+    unpack(0, lon_first[QUADS], lon_second[QUADS], 0)
+    unpack(last_row, lon_first[QUADS], lon_second[QUADS], 1)
+    for tc in range(ACROSS):
+        below, above = facing(lat, lat_first[tc], lat_second[tc])
+        hi_ref[tc + 1, 0] = above
+        hi_ref[tc + 1, last_row] = below
     mirror_copy.wait()
+    for copy in fields[:ACROSS]:
+        copy.wait()
 
     @pl.when(lat == 0)
     def _():
-        for tc in range(ACROSS):
-            nh[tc] = mirrored(hi_ref[tc, 0], 0)
+        for x in range(1, last_col):
+            hi_ref[x, 0] = mirrored(hi_ref[x, 1], 0)
 
     @pl.when(lat == 3)
     def _():
-        for tc in range(ACROSS):
-            sh[tc] = mirrored(hi_ref[tc, DOWN - 1], 1)
+        for x in range(1, last_col):
+            hi_ref[x, last_row] = mirrored(hi_ref[x, DOWN], 1)
 
     @pl.when(lon == 0)
     def _():
-        wh[0] = mirrored(nh[0], 2)
-        wh[1 : DOWN + 1] = mirrored(hi_ref[0], 2)
-        wh[DOWN + 1] = mirrored(sh[0], 2)
+        hi_ref[0] = mirrored(hi_ref[1], 2)
 
     @pl.when(lon == 31)
     def _():
-        eh[0] = mirrored(nh[ACROSS - 1], 3)
-        eh[1 : DOWN + 1] = mirrored(hi_ref[ACROSS - 1], 3)
-        eh[DOWN + 1] = mirrored(sh[ACROSS - 1], 3)
+        hi_ref[last_col] = mirrored(hi_ref[ACROSS], 3)
 
     @pl.when(lat == 0)
     def _():
-        wh[0] = mirrored(wh[1], 0)
-        eh[0] = mirrored(eh[1], 0)
+        for x in (0, last_col):
+            hi_ref[x, 0] = mirrored(hi_ref[x, 1], 0)
 
     @pl.when(lat == 3)
     def _():
-        wh[DOWN + 1] = mirrored(wh[DOWN], 1)
-        eh[DOWN + 1] = mirrored(eh[DOWN], 1)
-
-    lane = lax.broadcasted_iota(jnp.int32, flat, 1)
+        for x in (0, last_col):
+            hi_ref[x, last_row] = mirrored(hi_ref[x, DOWN], 1)
+
+    chunk = DIFFUSE_CHUNK
+    lane = lax.broadcasted_iota(jnp.int32, (chunk * SLOT_ROWS, CELLS), 1)
     upper = lane < 64
     east_side = jnp.bitwise_and(lane, 15) < 8
-    chunk = 8
-    zero = jnp.zeros(flat, jnp.bfloat16)
     weight_copy.wait()
 
+    stores = []
     for pair in range(ACROSS // 2):
         for part in range(DOWN // chunk):
-            total = None
-            for ref, is_hi in ((hi_ref, True), (lo_ref, False)):
-                if pair == 0 and part == 0 and not is_hi:
-                    for copy in fields:
-                        copy.wait()
-
-                def tile(x, tr):
-                    if x < 0 or x >= ACROSS:
-                        if not is_hi:
-                            return zero
-                        return (wh if x < 0 else eh)[tr + 1]
-                    if tr < 0 or tr >= DOWN:
-                        if not is_hi:
-                            return zero
-                        return (nh if tr < 0 else sh)[x]
-                    return ref[x, tr]
-
-                for k in range(chunk):
-                    tr = part * chunk + k
-                    own, both = [], []
-                    for x in range(2 * pair - 1, 2 * pair + 3):
-                        own.append(tile(x, tr))
-                        both.append(jnp.where(upper, tile(x, tr + 1), tile(x, tr - 1)))
-                    rows = slice(k * SLOT_ROWS, (k + 1) * SLOT_ROWS)
-                    left_ref[rows, 0:128] = own[1]
-                    left_ref[rows, 128:256] = own[2]
-                    left_ref[rows, 256:384] = jnp.where(east_side, own[3], own[0])
-                    left_ref[rows, 384:512] = both[1]
-                    left_ref[rows, 512:640] = both[2]
-                    left_ref[rows, 640:768] = jnp.where(east_side, both[3], both[0])
-                product = jnp.dot(left_ref[...], weight_ref[...], preferred_element_type=jnp.float32)
-                total = product if total is None else total + product
+            if pair == 0 and part == 0:
+                for copy in fields[ACROSS:]:
+                    copy.wait()
+
+            def rows(x, start):
+                return hi_ref[x, part * chunk + start : part * chunk + start + chunk].reshape(-1, CELLS)
+
+            own = [rows(x, 1) for x in range(2 * pair, 2 * pair + 4)]
+            both = [jnp.where(upper, rows(x, 2), rows(x, 0)) for x in range(2 * pair, 2 * pair + 4)]
+            left = jnp.concatenate(
+                [
+                    own[1],
+                    own[2],
+                    jnp.where(east_side, own[3], own[0]),
+                    both[1],
+                    both[2],
+                    jnp.where(east_side, both[3], both[0]),
+                ],
+                axis=1,
+            )
+            rest = [
+                lo_ref[2 * pair + u, part * chunk : part * chunk + chunk].reshape(-1, CELLS) for u in range(2)
+            ]
+            total = jnp.dot(left, weight_ref[...], preferred_element_type=jnp.float32)
+            total += jnp.dot(
+                jnp.concatenate(rest, axis=1), weight_ref[:256], preferred_element_type=jnp.float32
+            )
             for k in range(chunk):
                 tr = part * chunk + k
                 for u in range(2):
@@ -503,6 +498,12 @@
                     y = total[k * SLOT_ROWS : (k + 1) * SLOT_ROWS, u * 128 : (u + 1) * 128] * scale
                     inc_ref[tc, tr] = y
                     half_ref[tc * DOWN + tr] = y.astype(jnp.bfloat16)
+            for tc in (2 * pair, 2 * pair + 1):
+                block = pl.ds(part * chunk, chunk)
+                stores.append(
+                    pltpu.make_async_copy(inc_ref.at[tc, block], inc_hbm.at[tc, block], inc_sem.at[tc, part])
+                )
+                stores[-1].start()
 
     def answer(d, carry):
         reply_ref[d, :SLOT_ROWS, :] = half_ref[idx_ref[0, d]]
@@ -515,7 +516,7 @@
         part = pl.ds(32 * k, 32)
         copies.append(pltpu.make_async_copy(reply_ref.at[part], reply_hbm.at[part], reply_sem.at[k]))
         copies[-1].start()
-    for copy in copies:
+    for copy in stores + copies:
         copy.wait()
 
 
@@ -523,32 +524,29 @@
     vmem = pl.BlockSpec(memory_space=pltpu.VMEM)
     smem = pl.BlockSpec(memory_space=pltpu.SMEM)
     hbm = pl.BlockSpec(memory_space=pltpu.HBM)
+    ringed = (ACROSS + 2, DOWN + 2, SLOT_ROWS, CELLS)
+    block = (ACROSS, DOWN, SLOT_ROWS, CELLS)
     return pl.pallas_call(
         diffuse_kernel,
-        out_shape=(
-            jax.ShapeDtypeStruct((ACROSS, DOWN, SLOT_ROWS, CELLS), jnp.float32),
-            pltpu.HBM((128, 2 * SLOT_ROWS, CELLS), jnp.bfloat16),
-        ),
-        in_specs=[smem, smem, vmem, hbm] + [vmem] * 5 + [hbm] * 2,
-        out_specs=(vmem, hbm),
+        out_shape=(pltpu.HBM(block, jnp.float32), pltpu.HBM((128, 2 * SLOT_ROWS, CELLS), jnp.bfloat16)),
+        in_specs=[smem, smem, hbm, hbm] + [vmem] * 5 + [hbm] * 2,
+        out_specs=(hbm, hbm),
         scratch_shapes=[
-            pltpu.VMEM((ACROSS, DOWN, SLOT_ROWS, CELLS), jnp.bfloat16),
+            pltpu.VMEM(ringed, jnp.bfloat16),
+            pltpu.VMEM(block, jnp.bfloat16),
+            pltpu.VMEM(block, jnp.float32),
             pltpu.VMEM((TILES + 1, SLOT_ROWS, CELLS), jnp.bfloat16),
-            pltpu.VMEM((ACROSS, SLOT_ROWS, CELLS), jnp.bfloat16),
-            pltpu.VMEM((ACROSS, SLOT_ROWS, CELLS), jnp.bfloat16),
-            pltpu.VMEM((DOWN + 2, SLOT_ROWS, CELLS), jnp.bfloat16),
-            pltpu.VMEM((DOWN + 2, SLOT_ROWS, CELLS), jnp.bfloat16),
-            pltpu.VMEM((8 * SLOT_ROWS, 768), jnp.bfloat16),
             pltpu.VMEM((128, 2 * SLOT_ROWS, CELLS), jnp.bfloat16),
             pltpu.VMEM(weight.shape, weight.dtype),
             pltpu.VMEM(mirror.shape, mirror.dtype),
             pltpu.SemaphoreType.DMA((4,)),
             pltpu.SemaphoreType.DMA((2,)),
-            pltpu.SemaphoreType.DMA((ACROSS,)),
+            pltpu.SemaphoreType.DMA((2, ACROSS)),
+            pltpu.SemaphoreType.DMA((ACROSS, DOWN // DIFFUSE_CHUNK)),
         ],
         compiler_params=pltpu.CompilerParams(vmem_limit_bytes=32 * MIB),
         name="diffuse",
-    )(where, index, hi, in_hbm(lo), *halos, scale, in_hbm(weight), in_hbm(mirror))
+    )(where, index, in_hbm(hi), in_hbm(lo), *halos, scale, in_hbm(weight), in_hbm(mirror))
 
 
 def layout_kernel(inc_ref, out_ref, rows_ref):
@@ -597,20 +595,19 @@
 
 def forward_kernel(pos_ref, tiles_ref, foot_hbm, out_ref, foot, foot_sem):
     groups, slots, sounds, span = foot.shape
-    pairs = slots // 2
-
-    def fetch(g, j):
-        return pltpu.make_async_copy(foot_hbm.at[g, pl.ds(2 * j, 2)], foot.at[g, pl.ds(2 * j, 2)], foot_sem.at[g, j])
+
+    def fetch(g, first, last):
+        part = (g, pl.ds(first, last - first))
+        return pltpu.make_async_copy(foot_hbm.at[part], foot.at[part], foot_sem.at[g, first // LEAST])
 
     def start_group(g, carry):
-        for j in range(pairs):
-            if j < 3:
-                fetch(g, j).start()
-            else:
-
-                @pl.when(pos_ref[g * slots + 2 * j] >= 0)
-                def _():
-                    fetch(g, j).start()
+        fetch(g, 0, LEAST).start()
+        count = pos_ref[groups * slots + g]
+        for n in range(LEAST + 1, slots + 1):
+
+            @pl.when(count == n)
+            def _():
+                fetch(g, LEAST, n).start()
 
         return carry
 
@@ -618,25 +615,24 @@
 
     def group(g, carry):
         def one(j):
-            found = pos_ref[g * slots + j]
-            place = jnp.maximum(found, 0)
+            place = pos_ref[g * slots + j]
             at = pl.multiple_of(jnp.bitwise_and(place, 1) * SLOT_ROWS, SLOT_ROWS)
             tile = tiles_ref[lax.shift_right_logical(place, 1), pl.ds(at, SLOT_ROWS), :].astype(jnp.float32)
             left = jnp.concatenate([tile[w * 8 : w * 8 + 8] for w in range(WEEKS)], axis=1).astype(jnp.bfloat16)
-            value = lax.dot_general(
+            return lax.dot_general(
                 left, foot[g, j], (((1,), (1,)), ((), ())), preferred_element_type=jnp.float32
             )
-            return value if j < 6 else jnp.where(found >= 0, value, 0.0)
-
-        live = sum((pos_ref[g * slots + 2 * j] >= 0).astype(jnp.int32) for j in range(3, pairs)) + 3
-        for n in range(3, pairs + 1):
-
-            @pl.when(live == n)
+
+        count = pos_ref[groups * slots + g]
+        for n in range(LEAST, slots + 1):
+
+            @pl.when(count == n)
             def _():
-                for j in range(n):
-                    fetch(g, j).wait()
+                fetch(g, 0, LEAST).wait()
+                if n > LEAST:
+                    fetch(g, LEAST, n).wait()
                 total = one(0)
-                for j in range(1, 2 * n):
+                for j in range(1, n):
                     total = total + one(j)
                 out_ref[g] = total
 
@@ -656,7 +652,7 @@
         out_specs=vmem,
         scratch_shapes=[
             pltpu.VMEM(footprints.shape, footprints.dtype),
-            pltpu.SemaphoreType.DMA((groups, slots // 2)),
+            pltpu.SemaphoreType.DMA((groups, 2)),
         ],
         compiler_params=pltpu.CompilerParams(vmem_limit_bytes=32 * MIB),
         name="forward",

time: 126 us -> 122 us (0.968)
  Pallas kernels: 35.9 us -> 33.3 us
  local copies, waits for them, and re-layouts: 3.72 us -> 2.41 us
    pallas_call x2, Pallas kernels: 12.3 us -> 10.4 us  [the longest x1 5.59 us: diffuse_call(): pl.pallas_call(diffuse_kernel, out_shape=(pltpu.HBM(block, jnp.float32),...]
    unnamed x8 -> x6, local copies, waits for them, and re-layouts: 2.91 us -> 1.6 us
where the time goes in v2:
time: 122 us; the launch traced here: 121 us
  waiting for transfers between devices  58.5 us (48%)
  Pallas kernels  33.3 us (27%)
  starting transfers between devices  26.3 us (22%)
  local copies, waits for them, and re-layouts  2.41 us (2%)
    all_to_all x2, waiting for transfers between devices, exchanged(): lax.all_to_all(block, ('lat', 'lon'), split_axis=0, concat_axis=0, tiled=...  55.3 us
    all_to_all x2, starting transfers between devices, exchanged(): lax.all_to_all(block, ('lat', 'lon'), split_axis=0, concat_axis=0, tiled=...  24.2 us
    pallas_call x1, Pallas kernels, adjoint_call(): pl.pallas_call(adjoint_kernel, out_shape=(pltpu.HBM((128, SEND_ROWS, CELL...  8.44 us
    pallas_call x1, Pallas kernels, forward_call(): pl.pallas_call(forward_kernel, out_shape=jax.ShapeDtypeStruct((groups, PR...  8.05 us
    pallas_call x1, Pallas kernels, layout_call(): pl.pallas_call(layout_kernel, out_shape=jax.ShapeDtypeStruct((SLOT_ROWS *...  5.83 us
    pallas_call x1, Pallas kernels, diffuse_call(): pl.pallas_call(diffuse_kernel, out_shape=(pltpu.HBM(block, jnp.float32),...  5.59 us
    pallas_call x1, Pallas kernels, receive_call(): pl.pallas_call(receive_kernel, out_shape=(pltpu.HBM(block, jnp.bfloat16),...  4.78 us
    ppermute x1, waiting for transfers between devices, per_device(): lat_one = lax.ppermute(lat_one, 'lat', swaps(4, 0))  2.63 us
  transfers between devices with their start and end apart: 6, of which 4 were waited for; matrix products, arithmetic and copies ran while one was open for 1% of the time, Pallas kernels for 5%

profile of v2, /device:TPU:0, one launch (start us, length us, event | category | flops | bytes accessed | tf_op | source)
XLA Modules:
  0.0 121.4 jit_solution(1487268668236556386)
XLA Ops:
  0.6 8.4 %adjoint.1 = (bf16[128,72,128]{2,1,0:T(8,128)(2,1)}, s32[156]{0:T(256)S(1)}) custom-call(s32[12,12]{1,0:T(8,128)} %list_hbm.1, s32[12]{0:T(128)} %count_hbm.1, s32[16384]{0:T(1024)} %place_hbm.1, f32[12,8,128]{2,1,0:T(8,128)} %probe_hbm.1, f32[12,128]{1,0:T(8,128)} %prec_hbm.1, bf16[12,12,128,512]{3,2,1,0:T(8,128)(2,1)} %foot_hbm.3), custom_call_target="tpu_custom_call" | custom-call | tf_op jit(solution)/shard_map/adjoint/pallas_call | solution.py:197
  9.1 0.0 copy-start.1
  9.1 0.0 copy-start.2
  9.1 11.4 %all-to-all-start = ((bf16[128,72,128]{2,1,0:T(8,128)(2,1)}), bf16[128,72,128]{2,1,0:T(8,128)(2,1)S(1)}, u32[]{:S(2)}, u32[]{:S(2)}) async-start(bf16[128,72,128]{2,1,0:T(8,128)(2,1)} %get-tuple-element.16), calls=%async_computation | async-start | bytes 4718592 | tf_op jit(solution)/shard_map/all_to_all | solution.py:663
  20.5 0.0 copy-done.1
  20.5 0.0 copy-done.2
  20.5 0.1 copy.13
  20.6 0.3 reshape.13
  20.9 0.3 copy.14
  21.2 0.1 copy.15.scale_ref
  21.3 0.1 pad_add_fusion.where_ref
  21.4 32.3 %all-to-all-done.arr_ref = bf16[128,72,128]{2,1,0:T(8,128)(2,1)S(1)} async-done(((bf16[128,72,128]{2,1,0:T(8,128)(2,1)}), bf16[128,72,128]{2,1,0:T(8,128)(2,1)S(1)}, u32[]{:S(2)}, u32[]{:S(2)}) %all-to-all-start) | async-done | bytes 2359328 | tf_op jit(solution)/shard_map/all_to_all | solution.py:663
  53.7 4.8 %receive.1 = (bf16[4,32,32,128]{3,2,1,0:T(8,128)(2,1)}, bf16[4,32,32,128]{3,2,1,0:T(8,128)(2,1)}, bf16[4,32,128]{2,1,0:T(8,128)(2,1)S(1)}, bf16[4,32,128]{2,1,0:...) custom-call(s32[2]{0:T(128)S(1)} %pad_add_fusion.where_ref, ...), custom_call_target="tpu_custom_call" | custom-call | tf_op jit(solution)/shard_map/receive/pallas_call | solution.py:312
  58.5 0.7 collective-permute-start
  59.2 0.7 collective-permute-start.1
  59.9 2.6 %collective-permute-done.first_ref.lat_first = bf16[4,32,128]{2,1,0:T(8,128)(2,1)S(1)} collective-permute-done((bf16[4,32,128]{2,1,0:T(8,128)(2,1)S(1)}, bf16[4,32,128]{2,1,0:T(8,128)(2,1)S(1)}, u32[]{:S(2)}, u32[]{:S(2)}) %collective-permute-start) | collective-permute-done | bytes 32800 | tf_op jit(solution)/shard_map/ppermute | solution.py:683
  62.5 0.0 collective-permute-done.1.second_ref.lat_second
  62.5 0.6 corner.1
  63.1 0.1 collective-permute-start.2
  63.2 0.7 collective-permute-start.3
  63.9 0.6 collective-permute-done.2.lon_first
  64.5 0.0 collective-permute-done.3.lon_second
  64.5 5.6 %diffuse.1 = (f32[4,32,32,128]{3,2,1,0:T(8,128)}, bf16[128,64,128]{2,1,0:T(8,128)(2,1)}) custom-call(s32[2]{0:T(128)S(1)} %pad_add_fusion.where_ref, s32[8,128]{1,0:T(8,128)S(1)} %get-tuple-element.17.idx_ref, bf16[4,32,32,128]{3,2,1,0:T(8,128)(2,1)} %get-tuple-element.18.hi_hbm, bf16[4,32,32,128]{3,2,1,0:T(8,128)(2,1)} %get-tuple-element.19.lo_hbm, ...), custom_call_target="tpu_custom_call" | custom-call | tf_op jit(solution)/shard_map/diffuse/pallas_call | solution.py:529
  70.1 12.8 %all-to-all-start.1 = ((bf16[128,64,128]{2,1,0:T(8,128)(2,1)}), bf16[128,64,128]{2,1,0:T(8,128)(2,1)S(1)}, u32[]{:S(2)}, u32[]{:S(2)}) async-start(bf16[128,64,128]{2,1,0:T(8,128)(2,1)} %get-tuple-element.26), calls=%async_computation.1 | async-start | bytes 4194304 | tf_op jit(solution)/shard_map/all_to_all | solution.py:663
  82.9 0.0 copy-start
  82.9 1.6 %copy-done = f32[4,32,32,128]{3,2,1,0:T(8,128)S(1)} copy-done((f32[4,32,32,128]{3,2,1,0:T(8,128)S(1)}, f32[4,32,32,128]{3,2,1,0:T(8,128)}, u32[]{:S(2)}) %copy-start) | copy-done | bytes 2097176
  84.5 5.8 %layout.1 = f32[2048,256]{1,0:T(8,128)} custom-call(f32[4,32,32,128]{3,2,1,0:T(8,128)S(1)} %copy-done), custom_call_target="tpu_custom_call" | custom-call | flops 8388608 | bytes 8388608 | tf_op jit(solution)/shard_map/layout/pallas_call | solution.py:584
  90.3 23.0 %all-to-all-done.1.tiles_ref = bf16[128,64,128]{2,1,0:T(8,128)(2,1)S(1)} async-done(((bf16[128,64,128]{2,1,0:T(8,128)(2,1)}), bf16[128,64,128]{2,1,0:T(8,128)(2,1)S(1)}, u32[]{:S(2)}, u32[]{:S(2)}) %all-to-all-start.1) | async-done | bytes 2097184 | tf_op jit(solution)/shard_map/all_to_all | solution.py:663
  113.3 8.0 %forward.1 = f32[12,8,128]{2,1,0:T(8,128)} custom-call(s32[156]{0:T(256)S(1)} %get-tuple-element.15.pos_ref, bf16[128,64,128]{2,1,0:T(8,128)(2,1)S(1)} %all-to-all-done.1.tiles_ref, bf16[12,12,128,512]{3,2,1,0:T(8,128)(2,1)} %foot_hbm.3), custom_call_target="tpu_custom_call" | custom-call | tf_op jit(solution)/shard_map/forward/pallas_call | solution.py:648
  (1 shorter events, 0.0 us)
Async XLA Ops:
  9.1 11.4 %copy-start.1 = (f32[256,64]{0,1:T(8,128)S(1)}, f32[256,64]{0,1:T(8,128)}, u32[]{:S(2)}) copy-start(f32[256,64]{0,1:T(8,128)} %param.16) | copy-start | bytes 196612
  9.1 11.4 %copy-start.2 = (s32[256,64]{0,1:T(8,128)S(1)}, s32[256,64]{0,1:T(8,128)}, u32[]{:S(2)}) copy-start(s32[256,64]{0,1:T(8,128)} %param.17) | copy-start | bytes 196612
  9.1 44.6 %all-to-all-start = ((bf16[128,72,128]{2,1,0:T(8,128)(2,1)}), bf16[128,72,128]{2,1,0:T(8,128)(2,1)S(1)}, u32[]{:S(2)}, u32[]{:S(2)}) async-start(bf16[128,72,128]{2,1,0:T(8,128)(2,1)} %get-tuple-element.16), calls=%async_computation | async-start | bytes 4718592 | tf_op jit(solution)/shard_map/all_to_all | solution.py:663
  58.5 4.0 %collective-permute-start = (bf16[4,32,128]{2,1,0:T(8,128)(2,1)S(1)}, bf16[4,32,128]{2,1,0:T(8,128)(2,1)S(1)}, u32[]{:S(2)}, u32[]{:S(2)}) collective-permute-start(bf16[4,32,128]{2,1,0:T(8,128)(2,1)S(1)} %get-tuple-element.20), channel_id=1, source_target_pairs={{0,32},{64,96},{32,0},{96,64},{1,33},{65,97},{33,1},{97,65},{2,34}... | collective-permute-start | bytes 98312 | tf_op jit(solution)/shard_map/ppermute | solution.py:683
  59.2 3.3 %collective-permute-start.1 = (bf16[4,32,128]{2,1,0:T(8,128)(2,1)S(1)}, bf16[4,32,128]{2,1,0:T(8,128)(2,1)S(1)}, u32[]{:S(2)}, u32[]{:S(2)}) collective-permute-start(bf16[4,32,128]{2,1,0:T(8,128)(2,1)S(1)} %get-tuple-element.21), channel_id=1, source_target_pairs={{32,64},{64,32},{33,65},{65,33},{34,66},{66,34},{35,67},{67,35},{3... | collective-permute-start | bytes 98312 | tf_op jit(solution)/shard_map/ppermute | solution.py:684
  63.1 1.3 %collective-permute-start.2 = (bf16[9,32,128]{2,1,0:T(8,128)(2,1)S(1)}, bf16[9,32,128]{2,1,0:T(8,128)(2,1)S(1)}, u32[]{:S(2)}, u32[]{:S(2)}) collective-permute-start(bf16[9,32,128]{2,1,0:T(8,128)(2,1)S(1)} %get-tuple-element.24), channel_id=1, source_target_pairs={{0,1},{2,3},{4,5},{6,7},{8,9},{10,11},{12,13},{14,15},{16,17},{18,... | collective-permute-start | bytes 221192 | tf_op jit(solution)/shard_map/ppermute | solution.py:686
  63.2 1.3 %collective-permute-start.3 = (bf16[9,32,128]{2,1,0:T(8,128)(2,1)S(1)}, bf16[9,32,128]{2,1,0:T(8,128)(2,1)S(1)}, u32[]{:S(2)}, u32[]{:S(2)}) collective-permute-start(bf16[9,32,128]{2,1,0:T(8,128)(2,1)S(1)} %get-tuple-element.25), channel_id=1, source_target_pairs={{1,2},{3,4},{5,6},{7,8},{9,10},{11,12},{13,14},{15,16},{17,18},{19... | collective-permute-start | bytes 221192 | tf_op jit(solution)/shard_map/ppermute | solution.py:687
  70.1 43.3 %all-to-all-start.1 = ((bf16[128,64,128]{2,1,0:T(8,128)(2,1)}), bf16[128,64,128]{2,1,0:T(8,128)(2,1)S(1)}, u32[]{:S(2)}, u32[]{:S(2)}) async-start(bf16[128,64,128]{2,1,0:T(8,128)(2,1)} %get-tuple-element.26), calls=%async_computation.1 | async-start | bytes 4194304 | tf_op jit(solution)/shard_map/all_to_all | solution.py:663
  82.9 1.6 %copy-start = (f32[4,32,32,128]{3,2,1,0:T(8,128)S(1)}, f32[4,32,32,128]{3,2,1,0:T(8,128)}, u32[]{:S(2)}) copy-start(f32[4,32,32,128]{3,2,1,0:T(8,128)} %get-tuple-element.27.inc_ref) | copy-start | bytes 6291460

commit v3 on v2

--- a/solution.py
+++ b/solution.py
@@ -79,8 +79,8 @@
 
 
 def adjoint_kernel(
-    list_hbm, count_hbm, place_hbm, probe_hbm, prec_hbm, foot_hbm, out_hbm, pos_ref,
-    foot, packed, probe_ref, prec_ref, list_ref, count_ref, place_ref, seen_ref, small_sem, foot_sem, out_sem,
+    list_hbm, count_hbm, place_hbm, probe_hbm, prec_hbm, foot_hbm, out_hbm, pos_hbm,
+    foot, packed, probe_ref, prec_ref, pos_ref, list_ref, count_ref, place_ref, seen_ref, small_sem, foot_sem, out_sem, pos_sem,
 ):
     groups, slots = foot.shape[:2]
 
@@ -181,7 +181,8 @@
 
     lax.fori_loop(0, groups, group, 0)
 
-    copies = []
+    copies = [pltpu.make_async_copy(pos_ref, pos_hbm, pos_sem)]
+    copies[0].start()
     for k in range(4):
         part = pl.ds(32 * k, 32)
         copies.append(pltpu.make_async_copy(packed.at[part], out_hbm.at[part], out_sem.at[k]))
@@ -192,21 +193,21 @@
 
 def adjoint_call(tile_lists, counts, tile_place, probes, precision, footprints):
     groups, slots, sounds, span = footprints.shape
-    smem = pl.BlockSpec(memory_space=pltpu.SMEM)
     hbm = pl.BlockSpec(memory_space=pltpu.HBM)
     return pl.pallas_call(
         adjoint_kernel,
         out_shape=(
             pltpu.HBM((128, SEND_ROWS, CELLS), jnp.bfloat16),
-            jax.ShapeDtypeStruct((groups * slots + groups,), jnp.int32),
+            pltpu.HBM((groups * slots + groups,), jnp.int32),
         ),
         in_specs=[hbm] * 6,
-        out_specs=(hbm, smem),
+        out_specs=(hbm, hbm),
         scratch_shapes=[
             pltpu.VMEM((groups, slots, sounds, span), jnp.bfloat16),
             pltpu.VMEM((128, SEND_ROWS, CELLS), jnp.bfloat16),
             pltpu.VMEM(probes.shape, probes.dtype),
             pltpu.VMEM(precision.shape, precision.dtype),
+            pltpu.SMEM((groups * slots + groups,), jnp.int32),
             pltpu.SMEM(tile_lists.shape, jnp.int32),
             pltpu.SMEM(counts.shape, jnp.int32),
             pltpu.SMEM(tile_place.shape, jnp.int32),
@@ -214,6 +215,7 @@
             pltpu.SemaphoreType.DMA((5,)),
             pltpu.SemaphoreType.DMA((groups, 2)),
             pltpu.SemaphoreType.DMA((4,)),
+            pltpu.SemaphoreType.DMA,
         ],
         compiler_params=pltpu.CompilerParams(vmem_limit_bytes=32 * MIB),
         name="adjoint",
@@ -221,8 +223,8 @@
 
 
 def receive_kernel(
-    where_ref, arr_ref, scale_ref, hi_hbm, lo_hbm, first_ref, second_ref, west_ref, east_ref, idx_ref,
-    acc_a, acc_b, hi_ref, lo_ref, idx_vec, idx_sem, out_sem,
+    arr_ref, scale_ref, hi_hbm, lo_hbm, first_ref, second_ref, west_ref, east_ref, idx_vec,
+    acc_a, acc_b, hi_ref, lo_ref, idx_ref, idx_sem, out_sem,
 ):
     zero = jnp.zeros((SLOT_ROWS, CELLS), jnp.float32)
     lane8 = lax.broadcasted_iota(jnp.int32, (8, CELLS), 1)
@@ -256,7 +258,7 @@
     place = lax.shift_right_logical(jnp.bitwise_and(lane, 15), 2)
 
     copies = []
-    even = jnp.bitwise_and(where_ref[0], 1) == 0
+    even = jnp.bitwise_and(lax.axis_index("lat"), 1) == 0
     for tc in (1, 2, 0, 3):
 
         def finish(quad, carry):
@@ -302,10 +304,9 @@
         copy.wait()
 
 
-def receive_call(where, arrived, scale):
+def receive_call(arrived, scale):
     vmem = pl.BlockSpec(memory_space=pltpu.VMEM)
     hbm = pl.BlockSpec(memory_space=pltpu.HBM)
-    smem = pl.BlockSpec(memory_space=pltpu.SMEM)
     block = (ACROSS, DOWN, SLOT_ROWS, CELLS)
     row = jax.ShapeDtypeStruct((ACROSS, SLOT_ROWS, CELLS), jnp.bfloat16)
     column = jax.ShapeDtypeStruct((QUADS, SLOT_ROWS, CELLS), jnp.bfloat16)
@@ -320,20 +321,20 @@
             column,
             jax.ShapeDtypeStruct((8, 128), jnp.int32),
         ),
-        in_specs=[smem, vmem, vmem],
-        out_specs=(hbm, hbm) + (vmem,) * 4 + (smem,),
+        in_specs=[vmem, vmem],
+        out_specs=(hbm, hbm) + (vmem,) * 5,
         scratch_shapes=[
             pltpu.VMEM((TILES + 1, SLOT_ROWS, CELLS), jnp.float32),
             pltpu.VMEM((TILES + 1, SLOT_ROWS, CELLS), jnp.float32),
             pltpu.VMEM(block, jnp.bfloat16),
             pltpu.VMEM(block, jnp.bfloat16),
-            pltpu.VMEM((8, 128), jnp.int32),
+            pltpu.SMEM((8, 128), jnp.int32),
             pltpu.SemaphoreType.DMA,
             pltpu.SemaphoreType.DMA((2, ACROSS)),
         ],
         compiler_params=pltpu.CompilerParams(vmem_limit_bytes=24 * MIB),
         name="receive",
-    )(where, arrived, scale)
+    )(arrived, scale)
 
 
 def facing(flag, first, second):
@@ -341,10 +342,10 @@
     return jnp.where(even, first, second), jnp.where(even, second, first)
 
 
-def corner_kernel(where_ref, first_ref, second_ref, west_ref, east_ref, first_out, second_out):
+def corner_kernel(first_ref, second_ref, west_ref, east_ref, first_out, second_out):
     lane = lax.broadcasted_iota(jnp.int32, (SLOT_ROWS, CELLS), 1)
     place = lax.shift_right_logical(jnp.bitwise_and(lane, 15), 2)
-    even = jnp.bitwise_and(where_ref[1], 1) == 0
+    even = jnp.bitwise_and(lax.axis_index("lon"), 1) == 0
 
     def put(quad, west, east):
         first_out[quad] = jnp.where(even, east, west)
@@ -355,7 +356,7 @@
     corners = []
     for tc, shift in ((0, 0), (ACROSS - 1, 116)):
         below, above = facing(
-            where_ref[0], first_ref[tc].astype(jnp.float32), second_ref[tc].astype(jnp.float32)
+            lax.axis_index("lat"), first_ref[tc].astype(jnp.float32), second_ref[tc].astype(jnp.float32)
         )
         if shift:
             above = pltpu.roll(above, shift, 1)
@@ -364,27 +365,29 @@
     put(QUADS, *corners)
 
 
-def corner_call(where, first, second, west, east):
+def corner_call(first, second, west, east):
     vmem = pl.BlockSpec(memory_space=pltpu.VMEM)
     column = jax.ShapeDtypeStruct((QUADS + 1, SLOT_ROWS, CELLS), jnp.bfloat16)
     return pl.pallas_call(
         corner_kernel,
         out_shape=(column, column),
-        in_specs=[pl.BlockSpec(memory_space=pltpu.SMEM)] + [vmem] * 4,
+        in_specs=[vmem] * 4,
         out_specs=(vmem, vmem),
         compiler_params=pltpu.CompilerParams(vmem_limit_bytes=16 * MIB),
         name="corner",
-    )(where, first, second, west, east)
+    )(first, second, west, east)
 
 
 def diffuse_kernel(
-    where_ref, idx_ref, hi_hbm, lo_hbm, lat_first, lat_second, lon_first, lon_second,
+    idx_vec, hi_hbm, lo_hbm, lat_first, lat_second, lon_first, lon_second,
     scale_ref, weight_hbm, mirror_hbm,
     inc_hbm, reply_hbm,
-    hi_ref, lo_ref, inc_ref, half_ref, reply_ref, weight_ref, mirror_ref,
-    reply_sem, const_sem, field_sem, inc_sem,
+    hi_ref, lo_ref, inc_ref, half_ref, reply_ref, weight_ref, mirror_ref, idx_ref,
+    idx_sem, reply_sem, const_sem, field_sem, inc_sem,
 ):
-    lat, lon = where_ref[0], where_ref[1]
+    lat, lon = lax.axis_index("lat"), lax.axis_index("lon")
+    idx_copy = pltpu.make_async_copy(idx_vec, idx_ref, idx_sem)
+    idx_copy.start()
     last_row, last_col = DOWN + 1, ACROSS + 1
 
     def mirrored(block, side):
@@ -505,6 +508,8 @@
                 )
                 stores[-1].start()
 
+    idx_copy.wait()
+
     def answer(d, carry):
         reply_ref[d, :SLOT_ROWS, :] = half_ref[idx_ref[0, d]]
         reply_ref[d, SLOT_ROWS:, :] = half_ref[idx_ref[4, d]]
@@ -520,16 +525,15 @@
         copy.wait()
 
 
-def diffuse_call(where, index, hi, lo, halos, scale, weight, mirror):
+def diffuse_call(index, hi, lo, halos, scale, weight, mirror):
     vmem = pl.BlockSpec(memory_space=pltpu.VMEM)
-    smem = pl.BlockSpec(memory_space=pltpu.SMEM)
     hbm = pl.BlockSpec(memory_space=pltpu.HBM)
     ringed = (ACROSS + 2, DOWN + 2, SLOT_ROWS, CELLS)
     block = (ACROSS, DOWN, SLOT_ROWS, CELLS)
     return pl.pallas_call(
         diffuse_kernel,
         out_shape=(pltpu.HBM(block, jnp.float32), pltpu.HBM((128, 2 * SLOT_ROWS, CELLS), jnp.bfloat16)),
-        in_specs=[smem, smem, hbm, hbm] + [vmem] * 5 + [hbm] * 2,
+        in_specs=[vmem, hbm, hbm] + [vmem] * 5 + [hbm] * 2,
         out_specs=(hbm, hbm),
         scratch_shapes=[
             pltpu.VMEM(ringed, jnp.bfloat16),
@@ -539,6 +543,8 @@
             pltpu.VMEM((128, 2 * SLOT_ROWS, CELLS), jnp.bfloat16),
             pltpu.VMEM(weight.shape, weight.dtype),
             pltpu.VMEM(mirror.shape, mirror.dtype),
+            pltpu.SMEM((8, 128), jnp.int32),
+            pltpu.SemaphoreType.DMA,
             pltpu.SemaphoreType.DMA((4,)),
             pltpu.SemaphoreType.DMA((2,)),
             pltpu.SemaphoreType.DMA((2, ACROSS)),
@@ -546,7 +552,7 @@
         ],
         compiler_params=pltpu.CompilerParams(vmem_limit_bytes=32 * MIB),
         name="diffuse",
-    )(where, index, in_hbm(hi), in_hbm(lo), *halos, scale, in_hbm(weight), in_hbm(mirror))
+    )(index, in_hbm(hi), in_hbm(lo), *halos, scale, in_hbm(weight), in_hbm(mirror))
 
 
 def layout_kernel(inc_ref, out_ref, rows_ref):
@@ -593,15 +599,24 @@
     )(inc)
 
 
-def forward_kernel(pos_ref, tiles_ref, foot_hbm, out_ref, foot, foot_sem):
+def forward_kernel(pos_hbm, tiles_ref, foot_hbm, out_ref, foot, pos_ref, pos_sem, foot_sem):
     groups, slots, sounds, span = foot.shape
 
     def fetch(g, first, last):
         part = (g, pl.ds(first, last - first))
         return pltpu.make_async_copy(foot_hbm.at[part], foot.at[part], foot_sem.at[g, first // LEAST])
 
+    pos_copy = pltpu.make_async_copy(pos_hbm, pos_ref, pos_sem)
+    pos_copy.start()
+    fetch(0, 0, LEAST).start()
+    fetch(1, 0, LEAST).start()
+    pos_copy.wait()
+
     def start_group(g, carry):
-        fetch(g, 0, LEAST).start()
+        @pl.when(g > 1)
+        def _():
+            fetch(g, 0, LEAST).start()
+
         count = pos_ref[groups * slots + g]
         for n in range(LEAST + 1, slots + 1):
 
@@ -643,20 +658,22 @@
 
 def forward_call(pos, tiles, footprints):
     groups, slots, sounds, span = footprints.shape
-    smem = pl.BlockSpec(memory_space=pltpu.SMEM)
+    hbm = pl.BlockSpec(memory_space=pltpu.HBM)
     vmem = pl.BlockSpec(memory_space=pltpu.VMEM)
     return pl.pallas_call(
         forward_kernel,
         out_shape=jax.ShapeDtypeStruct((groups, PROBES, sounds), jnp.float32),
-        in_specs=[smem, vmem, pl.BlockSpec(memory_space=pltpu.HBM)],
+        in_specs=[hbm, vmem, hbm],
         out_specs=vmem,
         scratch_shapes=[
             pltpu.VMEM(footprints.shape, footprints.dtype),
+            pltpu.SMEM(pos.shape, jnp.int32),
+            pltpu.SemaphoreType.DMA,
             pltpu.SemaphoreType.DMA((groups, 2)),
         ],
         compiler_params=pltpu.CompilerParams(vmem_limit_bytes=32 * MIB),
         name="forward",
-    )(pos, tiles, in_hbm(footprints))
+    )(in_hbm(pos), tiles, in_hbm(footprints))
 
 
 def exchanged(block):
@@ -671,25 +688,23 @@
 def per_device(
     footprints, tile_lists, tile_counts, tile_place, probes, obs_precision, prior_sigma, land_mask
 ):
-    lat, lon = lax.axis_index("lat"), lax.axis_index("lon")
     outgoing, pos = adjoint_call(tile_lists, tile_counts, tile_place, probes, obs_precision, footprints)
     arrived = exchanged(outgoing)
 
     scale = prior_sigma * land_mask.astype(jnp.float32)
     scale = scale.reshape(DOWN, TILE_ROWS, ACROSS, TILE_COLS).transpose(2, 0, 1, 3).reshape(ACROSS, DOWN, CELLS)
 
-    where = jnp.stack([lat, lon]).astype(jnp.int32)
-    hi, lo, lat_one, lat_two, left, right, index = receive_call(where, arrived, scale)
+    hi, lo, lat_one, lat_two, left, right, index = receive_call(arrived, scale)
     lat_one = lax.ppermute(lat_one, "lat", swaps(4, 0))
     lat_two = lax.ppermute(lat_two, "lat", swaps(4, 1))
-    lon_one, lon_two = corner_call(where, lat_one, lat_two, left, right)
+    lon_one, lon_two = corner_call(lat_one, lat_two, left, right)
     lon_one = lax.ppermute(lon_one, "lon", swaps(32, 0))
     lon_two = lax.ppermute(lon_two, "lon", swaps(32, 1))
     halos = (lat_one, lat_two, lon_one, lon_two)
 
     weight = jnp.asarray(stencil_weights(), jnp.bfloat16)
     mirror = jnp.asarray(reflections(), jnp.bfloat16)
-    inc, reply = diffuse_call(where, index, hi, lo, halos, scale, weight, mirror)
+    inc, reply = diffuse_call(index, hi, lo, halos, scale, weight, mirror)
     returned = exchanged(reply)
     increment = layout_call(inc).reshape(SLOT_ROWS, 64, 256).transpose(2, 0, 1)
     predicted = forward_call(pos, returned, footprints)

time: 122 us -> 119 us (0.975)
  Pallas kernels: 33.3 us -> 30.5 us
    pallas_call x1, Pallas kernels: 4.78 us -> 3.56 us  [receive_call(): pl.pallas_call(receive_kernel, out_shape=(pltpu.HBM(block, jnp.bfloat16),...]
where the time goes in v3:
time: 119 us; the launch traced here: 118 us
  waiting for transfers between devices  58.6 us (49%)
  Pallas kernels  30.5 us (26%)
  starting transfers between devices  26.1 us (22%)
  local copies, waits for them, and re-layouts  2.39 us (2%)
    all_to_all x2, waiting for transfers between devices, exchanged(): lax.all_to_all(block, ('lat', 'lon'), split_axis=0, concat_axis=0, tiled=...  55.4 us
    all_to_all x2, starting transfers between devices, exchanged(): lax.all_to_all(block, ('lat', 'lon'), split_axis=0, concat_axis=0, tiled=...  24 us
    pallas_call x1, Pallas kernels, forward_call(): pl.pallas_call(forward_kernel, out_shape=jax.ShapeDtypeStruct((groups, PR...  8.15 us
    pallas_call x1, Pallas kernels, adjoint_call(): pl.pallas_call(adjoint_kernel, out_shape=(pltpu.HBM((128, SEND_ROWS, CELL...  7.89 us
    pallas_call x1, Pallas kernels, layout_call(): pl.pallas_call(layout_kernel, out_shape=jax.ShapeDtypeStruct((SLOT_ROWS *...  5.83 us
    pallas_call x1, Pallas kernels, diffuse_call(): pl.pallas_call(diffuse_kernel, out_shape=(pltpu.HBM(block, jnp.float32),...  5 us
    pallas_call x1, Pallas kernels, receive_call(): pl.pallas_call(receive_kernel, out_shape=(pltpu.HBM(block, jnp.bfloat16),...  3.56 us
    ppermute x1, waiting for transfers between devices, per_device(): lat_one = lax.ppermute(lat_one, 'lat', swaps(4, 0))  2.6 us
  transfers between devices with their start and end apart: 6, of which 4 were waited for; matrix products, arithmetic and copies ran while one was open for 1% of the time, Pallas kernels for 5%

profile of v3, /device:TPU:0, one launch (start us, length us, event | category | flops | bytes accessed | tf_op | source)
XLA Modules:
  0.0 118.3 jit_solution(6147614250275408319)
XLA Ops:
  0.6 7.9 %adjoint.1 = (bf16[128,72,128]{2,1,0:T(8,128)(2,1)}, s32[156]{0:T(256)}) custom-call(s32[12,12]{1,0:T(8,128)} %list_hbm.1, s32[12]{0:T(128)} %count_hbm.1, s32[16384]{0:T(1024)} %place_hbm.1, f32[12,8,128]{2,1,0:T(8,128)} %probe_hbm.1, f32[12,128]{1,0:T(8,128)} %prec_hbm.1, bf16[12,12,128,512]{3,2,1,0:T(8,128)(2,1)} %foot_hbm.3), custom_call_target="tpu_custom_call" | custom-call | tf_op jit(solution)/shard_map/adjoint/pallas_call | solution.py:197
  8.5 0.0 copy-start.1
  8.5 0.0 copy-start.2
  8.6 11.1 %all-to-all-start = ((bf16[128,72,128]{2,1,0:T(8,128)(2,1)}), bf16[128,72,128]{2,1,0:T(8,128)(2,1)S(1)}, u32[]{:S(2)}, u32[]{:S(2)}) async-start(bf16[128,72,128]{2,1,0:T(8,128)(2,1)} %get-tuple-element.16), calls=%async_computation | async-start | bytes 4718592 | tf_op jit(solution)/shard_map/all_to_all | solution.py:680
  19.7 0.0 copy-done.1
  19.7 0.0 copy-done.2
  19.7 0.1 copy.13
  19.8 0.3 reshape.13
  20.1 0.3 copy.14
  20.4 0.1 copy.15.scale_ref
  20.5 32.4 %all-to-all-done.arr_ref = bf16[128,72,128]{2,1,0:T(8,128)(2,1)S(1)} async-done(((bf16[128,72,128]{2,1,0:T(8,128)(2,1)}), bf16[128,72,128]{2,1,0:T(8,128)(2,1)S(1)}, u32[]{:S(2)}, u32[]{:S(2)}) %all-to-all-start) | async-done | bytes 2359328 | tf_op jit(solution)/shard_map/all_to_all | solution.py:680
  52.9 3.6 %receive.1 = (bf16[4,32,32,128]{3,2,1,0:T(8,128)(2,1)}, bf16[4,32,32,128]{3,2,1,0:T(8,128)(2,1)}, bf16[4,32,128]{2,1,0:T(8,128)(2,1)S(1)}, bf16[4,32,128]{2,1,0:...) custom-call(bf16[128,72,128]{2,1,0:T(8,128)(2,1)S(1)} %all-to-all-done.arr, ...), custom_call_target="tpu_custom_call" | custom-call | tf_op jit(solution)/shard_map/receive/pallas_call | solution.py:313
  56.5 0.7 collective-permute-start
  57.2 0.7 collective-permute-start.1
  57.9 2.6 %collective-permute-done.first_ref.lat_first = bf16[4,32,128]{2,1,0:T(8,128)(2,1)S(1)} collective-permute-done((bf16[4,32,128]{2,1,0:T(8,128)(2,1)S(1)}, bf16[4,32,128]{2,1,0:T(8,128)(2,1)S(1)}, u32[]{:S(2)}, u32[]{:S(2)}) %collective-permute-start) | collective-permute-done | bytes 32800 | tf_op jit(solution)/shard_map/ppermute | solution.py:698
  60.5 0.0 collective-permute-done.1.second_ref.lat_second
  60.5 0.1 corner.1
  60.6 0.1 collective-permute-start.2
  60.6 0.7 collective-permute-start.3
  61.3 0.6 collective-permute-done.2.lon_first
  61.9 0.0 collective-permute-done.3.lon_second
  61.9 5.0 %diffuse.1 = (f32[4,32,32,128]{3,2,1,0:T(8,128)}, bf16[128,64,128]{2,1,0:T(8,128)(2,1)}) custom-call(s32[8,128]{1,0:T(8,128)S(1)} %get-tuple-element.17.idx_vec, bf16[4,32,32,128]{3,2,1,0:T(8,128)(2,1)} %get-tuple-element.18.hi_hbm, bf16[4,32,32,128]{3,2,1,0:T(8,128)(2,1)} %get-tuple-element.19.lo_hbm, ...), custom_call_target="tpu_custom_call" | custom-call | tf_op jit(solution)/shard_map/diffuse/pallas_call | solution.py:533
  66.9 12.8 %all-to-all-start.1 = ((bf16[128,64,128]{2,1,0:T(8,128)(2,1)}), bf16[128,64,128]{2,1,0:T(8,128)(2,1)S(1)}, u32[]{:S(2)}, u32[]{:S(2)}) async-start(bf16[128,64,128]{2,1,0:T(8,128)(2,1)} %get-tuple-element.26), calls=%async_computation.1 | async-start | bytes 4194304 | tf_op jit(solution)/shard_map/all_to_all | solution.py:680
  79.7 0.0 copy-start
  79.8 1.6 %copy-done = f32[4,32,32,128]{3,2,1,0:T(8,128)S(1)} copy-done((f32[4,32,32,128]{3,2,1,0:T(8,128)S(1)}, f32[4,32,32,128]{3,2,1,0:T(8,128)}, u32[]{:S(2)}) %copy-start) | copy-done | bytes 2097176
  81.3 5.8 %layout.1 = f32[2048,256]{1,0:T(8,128)} custom-call(f32[4,32,32,128]{3,2,1,0:T(8,128)S(1)} %copy-done), custom_call_target="tpu_custom_call" | custom-call | flops 8388608 | bytes 8388608 | tf_op jit(solution)/shard_map/layout/pallas_call | solution.py:590
  87.2 23.0 %all-to-all-done.1.tiles_ref = bf16[128,64,128]{2,1,0:T(8,128)(2,1)S(1)} async-done(((bf16[128,64,128]{2,1,0:T(8,128)(2,1)}), bf16[128,64,128]{2,1,0:T(8,128)(2,1)S(1)}, u32[]{:S(2)}, u32[]{:S(2)}) %all-to-all-start.1) | async-done | bytes 2097184 | tf_op jit(solution)/shard_map/all_to_all | solution.py:680
  110.2 8.2 %forward.1 = f32[12,8,128]{2,1,0:T(8,128)} custom-call(s32[156]{0:T(256)} %get-tuple-element.15.pos_hbm, bf16[128,64,128]{2,1,0:T(8,128)(2,1)S(1)} %all-to-all-done.1.tiles_ref, bf16[12,12,128,512]{3,2,1,0:T(8,128)(2,1)} %foot_hbm.3), custom_call_target="tpu_custom_call" | custom-call | tf_op jit(solution)/shard_map/forward/pallas_call | solution.py:663
  (1 shorter events, 0.0 us)
Async XLA Ops:
  8.5 11.1 %copy-start.1 = (f32[256,64]{0,1:T(8,128)S(1)}, f32[256,64]{0,1:T(8,128)}, u32[]{:S(2)}) copy-start(f32[256,64]{0,1:T(8,128)} %param.16) | copy-start | bytes 196612
  8.5 11.1 %copy-start.2 = (s32[256,64]{0,1:T(8,128)S(1)}, s32[256,64]{0,1:T(8,128)}, u32[]{:S(2)}) copy-start(s32[256,64]{0,1:T(8,128)} %param.17) | copy-start | bytes 196612
  8.6 44.3 %all-to-all-start = ((bf16[128,72,128]{2,1,0:T(8,128)(2,1)}), bf16[128,72,128]{2,1,0:T(8,128)(2,1)S(1)}, u32[]{:S(2)}, u32[]{:S(2)}) async-start(bf16[128,72,128]{2,1,0:T(8,128)(2,1)} %get-tuple-element.16), calls=%async_computation | async-start | bytes 4718592 | tf_op jit(solution)/shard_map/all_to_all | solution.py:680
  56.5 4.0 %collective-permute-start = (bf16[4,32,128]{2,1,0:T(8,128)(2,1)S(1)}, bf16[4,32,128]{2,1,0:T(8,128)(2,1)S(1)}, u32[]{:S(2)}, u32[]{:S(2)}) collective-permute-start(bf16[4,32,128]{2,1,0:T(8,128)(2,1)S(1)} %get-tuple-element.20), channel_id=1, source_target_pairs={{0,32},{64,96},{32,0},{96,64},{1,33},{65,97},{33,1},{97,65},{2,34}... | collective-permute-start | bytes 98312 | tf_op jit(solution)/shard_map/ppermute | solution.py:698
  57.2 3.3 %collective-permute-start.1 = (bf16[4,32,128]{2,1,0:T(8,128)(2,1)S(1)}, bf16[4,32,128]{2,1,0:T(8,128)(2,1)S(1)}, u32[]{:S(2)}, u32[]{:S(2)}) collective-permute-start(bf16[4,32,128]{2,1,0:T(8,128)(2,1)S(1)} %get-tuple-element.21), channel_id=1, source_target_pairs={{32,64},{64,32},{33,65},{65,33},{34,66},{66,34},{35,67},{67,35},{3... | collective-permute-start | bytes 98312 | tf_op jit(solution)/shard_map/ppermute | solution.py:699
  60.6 1.3 %collective-permute-start.2 = (bf16[9,32,128]{2,1,0:T(8,128)(2,1)S(1)}, bf16[9,32,128]{2,1,0:T(8,128)(2,1)S(1)}, u32[]{:S(2)}, u32[]{:S(2)}) collective-permute-start(bf16[9,32,128]{2,1,0:T(8,128)(2,1)S(1)} %get-tuple-element.24), channel_id=1, source_target_pairs={{0,1},{2,3},{4,5},{6,7},{8,9},{10,11},{12,13},{14,15},{16,17},{18,... | collective-permute-start | bytes 221192 | tf_op jit(solution)/shard_map/ppermute | solution.py:701
  60.6 1.3 %collective-permute-start.3 = (bf16[9,32,128]{2,1,0:T(8,128)(2,1)S(1)}, bf16[9,32,128]{2,1,0:T(8,128)(2,1)S(1)}, u32[]{:S(2)}, u32[]{:S(2)}) collective-permute-start(bf16[9,32,128]{2,1,0:T(8,128)(2,1)S(1)} %get-tuple-element.25), channel_id=1, source_target_pairs={{1,2},{3,4},{5,6},{7,8},{9,10},{11,12},{13,14},{15,16},{17,18},{19... | collective-permute-start | bytes 221192 | tf_op jit(solution)/shard_map/ppermute | solution.py:702
  66.9 43.3 %all-to-all-start.1 = ((bf16[128,64,128]{2,1,0:T(8,128)(2,1)}), bf16[128,64,128]{2,1,0:T(8,128)(2,1)S(1)}, u32[]{:S(2)}, u32[]{:S(2)}) async-start(bf16[128,64,128]{2,1,0:T(8,128)(2,1)} %get-tuple-element.26), calls=%async_computation.1 | async-start | bytes 4194304 | tf_op jit(solution)/shard_map/all_to_all | solution.py:680
  79.7 1.6 %copy-start = (f32[4,32,32,128]{3,2,1,0:T(8,128)S(1)}, f32[4,32,32,128]{3,2,1,0:T(8,128)}, u32[]{:S(2)}) copy-start(f32[4,32,32,128]{3,2,1,0:T(8,128)} %get-tuple-element.27.inc_ref) | copy-start | bytes 6291460

commit v4 on v3

--- a/solution.py
+++ b/solution.py
@@ -21,6 +21,7 @@
 SEND_ROWS = 2 * SLOT_ROWS + 8
 QUADS = DOWN // 4
 DIFFUSE_CHUNK = 8
+AHEAD = 4
 LEAST = 6
 
 diffusion_rate = 0.2
@@ -117,15 +118,17 @@
 
         return carry
 
-    start_sure(0, 0)
+    for g in range(AHEAD):
+        start_sure(g, 0)
     small[0].wait()
-    start_rest(0, 0)
+    for g in range(AHEAD):
+        start_rest(g, 0)
 
     def start_group(g, carry):
         start_sure(g, carry)
         return start_rest(g, carry)
 
-    lax.fori_loop(1, groups, start_group, 0)
+    lax.fori_loop(AHEAD, groups, start_group, 0)
 
     nobody = jnp.full((8, CELLS), TILES, jnp.float32).astype(jnp.bfloat16)
     number_row = lax.shift_right_logical(lax.broadcasted_iota(jnp.int32, (8, CELLS), 0), 2)
@@ -252,7 +255,7 @@
         acc_b[ib] += arr_ref[d, SLOT_ROWS : 2 * SLOT_ROWS, :].astype(jnp.float32)
         return carry
 
-    lax.fori_loop(0, 128, add, 0, unroll=8)
+    lax.fori_loop(0, 128, add, 0, unroll=16)
 
     lane = lax.broadcasted_iota(jnp.int32, (SLOT_ROWS, CELLS), 1)
     place = lax.shift_right_logical(jnp.bitwise_and(lane, 15), 2)
@@ -291,7 +294,7 @@
                 east_ref[quad] = edge.astype(jnp.bfloat16)
             return carry
 
-        lax.fori_loop(0, QUADS, finish, 0, unroll=2)
+        lax.fori_loop(0, QUADS, finish, 0, unroll=4)
         top = hi_ref[tc, 0]
         bottom = hi_ref[tc, DOWN - 1]
         first_ref[tc] = jnp.where(even, bottom, top)
@@ -342,7 +345,7 @@
     return jnp.where(even, first, second), jnp.where(even, second, first)
 
 
-def corner_kernel(first_ref, second_ref, west_ref, east_ref, first_out, second_out):
+def corner_kernel(first_ref, second_ref, west_ref, east_ref, second_out, first_out):
     lane = lax.broadcasted_iota(jnp.int32, (SLOT_ROWS, CELLS), 1)
     place = lax.shift_right_logical(jnp.bitwise_and(lane, 15), 2)
     even = jnp.bitwise_and(lax.axis_index("lon"), 1) == 0
@@ -379,7 +382,7 @@
 
 
 def diffuse_kernel(
-    idx_vec, hi_hbm, lo_hbm, lat_first, lat_second, lon_first, lon_second,
+    idx_vec, hi_hbm, lo_hbm, lat_first, lat_second, lon_second, lon_first,
     scale_ref, weight_hbm, mirror_hbm,
     inc_hbm, reply_hbm,
     hi_ref, lo_ref, inc_ref, half_ref, reply_ref, weight_ref, mirror_ref, idx_ref,
@@ -418,7 +421,7 @@
             unpack(i, lon_first[quad], lon_second[quad], k)
         return carry
 
-    lax.fori_loop(0, QUADS, unpack_quad, 0, unroll=2)
+    lax.fori_loop(0, QUADS, unpack_quad, 0, unroll=4)
     unpack(0, lon_first[QUADS], lon_second[QUADS], 0)
     unpack(last_row, lon_first[QUADS], lon_second[QUADS], 1)
     for tc in range(ACROSS):
@@ -608,12 +611,12 @@
 
     pos_copy = pltpu.make_async_copy(pos_hbm, pos_ref, pos_sem)
     pos_copy.start()
-    fetch(0, 0, LEAST).start()
-    fetch(1, 0, LEAST).start()
+    for g in range(AHEAD):
+        fetch(g, 0, LEAST).start()
     pos_copy.wait()
 
     def start_group(g, carry):
-        @pl.when(g > 1)
+        @pl.when(g >= AHEAD)
         def _():
             fetch(g, 0, LEAST).start()
 
@@ -697,10 +700,10 @@
     hi, lo, lat_one, lat_two, left, right, index = receive_call(arrived, scale)
     lat_one = lax.ppermute(lat_one, "lat", swaps(4, 0))
     lat_two = lax.ppermute(lat_two, "lat", swaps(4, 1))
-    lon_one, lon_two = corner_call(lat_one, lat_two, left, right)
+    lon_two, lon_one = corner_call(lat_one, lat_two, left, right)
+    lon_two = lax.ppermute(lon_two, "lon", swaps(32, 1))
     lon_one = lax.ppermute(lon_one, "lon", swaps(32, 0))
-    lon_two = lax.ppermute(lon_two, "lon", swaps(32, 1))
-    halos = (lat_one, lat_two, lon_one, lon_two)
+    halos = (lat_one, lat_two, lon_two, lon_one)
 
     weight = jnp.asarray(stencil_weights(), jnp.bfloat16)
     mirror = jnp.asarray(reflections(), jnp.bfloat16)

time: 119 us -> 118 us (level)
    all_to_all x2, starting transfers between devices: 24 us -> 21.8 us  [exchanged(): lax.all_to_all(block, ('lat', 'lon'), split_axis=0, concat_axis=0, tiled=...]
    ppermute x1, starting transfers between devices: 0.07 us -> 1.72 us  [per_device(): lon_one = lax.ppermute(lon_one, 'lon', swaps(32, 0))]
where the time goes in v4:
time: 118 us
  waiting for transfers between devices  58.9 us (50%)
  Pallas kernels  30.3 us (26%)
  starting transfers between devices  25.5 us (22%)
  local copies, waits for them, and re-layouts  2.39 us (2%)
    all_to_all x2, waiting for transfers between devices, exchanged(): lax.all_to_all(block, ('lat', 'lon'), split_axis=0, concat_axis=0, tiled=...  55.4 us
    all_to_all x2, starting transfers between devices, exchanged(): lax.all_to_all(block, ('lat', 'lon'), split_axis=0, concat_axis=0, tiled=...  21.8 us
    pallas_call x1, Pallas kernels, forward_call(): pl.pallas_call(forward_kernel, out_shape=jax.ShapeDtypeStruct((groups, PR...  8.3 us
    pallas_call x1, Pallas kernels, adjoint_call(): pl.pallas_call(adjoint_kernel, out_shape=(pltpu.HBM((128, SEND_ROWS, CELL...  7.87 us
    pallas_call x1, Pallas kernels, layout_call(): pl.pallas_call(layout_kernel, out_shape=jax.ShapeDtypeStruct((SLOT_ROWS *...  5.83 us
    pallas_call x1, Pallas kernels, diffuse_call(): pl.pallas_call(diffuse_kernel, out_shape=(pltpu.HBM(block, jnp.float32),...  4.99 us
    pallas_call x1, Pallas kernels, receive_call(): pl.pallas_call(receive_kernel, out_shape=(pltpu.HBM(block, jnp.bfloat16),...  3.24 us
    ppermute x1, waiting for transfers between devices, per_device(): lat_one = lax.ppermute(lat_one, 'lat', swaps(4, 0))  2.62 us
  transfers between devices with their start and end apart: 6, of which 4 were waited for; matrix products, arithmetic and copies ran while one was open for 1% of the time, Pallas kernels for 5%

profile of v4, /device:TPU:0, one launch (start us, length us, event | category | flops | bytes accessed | tf_op | source)
XLA Modules:
  0.0 117.9 jit_solution(10550733245918329414)
XLA Ops:
  0.6 7.9 %adjoint.1 = (bf16[128,72,128]{2,1,0:T(8,128)(2,1)}, s32[156]{0:T(256)}) custom-call(s32[12,12]{1,0:T(8,128)} %list_hbm.1, s32[12]{0:T(128)} %count_hbm.1, s32[16384]{0:T(1024)} %place_hbm.1, f32[12,8,128]{2,1,0:T(8,128)} %probe_hbm.1, f32[12,128]{1,0:T(8,128)} %prec_hbm.1, bf16[12,12,128,512]{3,2,1,0:T(8,128)(2,1)} %foot_hbm.3), custom_call_target="tpu_custom_call" | custom-call | tf_op jit(solution)/shard_map/adjoint/pallas_call | solution.py:200
  8.5 0.0 copy-start.1
  8.5 0.0 copy-start.2
  8.5 11.0 %all-to-all-start = ((bf16[128,72,128]{2,1,0:T(8,128)(2,1)}), bf16[128,72,128]{2,1,0:T(8,128)(2,1)S(1)}, u32[]{:S(2)}, u32[]{:S(2)}) async-start(bf16[128,72,128]{2,1,0:T(8,128)(2,1)} %get-tuple-element.16), calls=%async_computation | async-start | bytes 4718592 | tf_op jit(solution)/shard_map/all_to_all | solution.py:683
  19.5 0.0 copy-done.1
  19.5 0.0 copy-done.2
  19.5 0.1 copy.13
  19.6 0.3 reshape.13
  19.9 0.3 copy.14
  20.2 0.1 copy.15.scale_ref
  20.4 32.4 %all-to-all-done.arr_ref = bf16[128,72,128]{2,1,0:T(8,128)(2,1)S(1)} async-done(((bf16[128,72,128]{2,1,0:T(8,128)(2,1)}), bf16[128,72,128]{2,1,0:T(8,128)(2,1)S(1)}, u32[]{:S(2)}, u32[]{:S(2)}) %all-to-all-start) | async-done | bytes 2359328 | tf_op jit(solution)/shard_map/all_to_all | solution.py:683
  52.7 3.2 %receive.1 = (bf16[4,32,32,128]{3,2,1,0:T(8,128)(2,1)}, bf16[4,32,32,128]{3,2,1,0:T(8,128)(2,1)}, bf16[4,32,128]{2,1,0:T(8,128)(2,1)S(1)}, bf16[4,32,128]{2,1,0:...) custom-call(bf16[128,72,128]{2,1,0:T(8,128)(2,1)S(1)} %all-to-all-done.arr, ...), custom_call_target="tpu_custom_call" | custom-call | tf_op jit(solution)/shard_map/receive/pallas_call | solution.py:316
  56.0 0.7 collective-permute-start
  56.7 0.7 collective-permute-start.1
  57.4 2.6 %collective-permute-done.first_ref.lat_first = bf16[4,32,128]{2,1,0:T(8,128)(2,1)S(1)} collective-permute-done((bf16[4,32,128]{2,1,0:T(8,128)(2,1)S(1)}, bf16[4,32,128]{2,1,0:T(8,128)(2,1)S(1)}, u32[]{:S(2)}, u32[]{:S(2)}) %collective-permute-start) | collective-permute-done | bytes 32800 | tf_op jit(solution)/shard_map/ppermute | solution.py:701
  60.0 0.0 collective-permute-done.1.second_ref.lat_second
  60.0 0.1 corner.1
  60.1 0.7 collective-permute-start.2
  60.7 1.7 %collective-permute-start.3 = (bf16[9,32,128]{2,1,0:T(8,128)(2,1)S(1)}, bf16[9,32,128]{2,1,0:T(8,128)(2,1)S(1)}, u32[]{:S(2)}, u32[]{:S(2)}) collective-permute-start(bf16[9,32,128]{2,1,0:T(8,128)(2,1)S(1)} %get-tuple-element.25), channel_id=1, source_target_pairs={{0,1},{2,3},{4,5},{6,7},{8,9},{10,11},{12,13},{14,15},{16,17},{18,... | collective-permute-start | bytes 221192 | tf_op jit(solution)/shard_map/ppermute | solution.py:705
  62.4 0.0 collective-permute-done.2.lon_second
  62.4 0.9 collective-permute-done.3.lon_first
  63.4 5.0 %diffuse.1 = (f32[4,32,32,128]{3,2,1,0:T(8,128)}, bf16[128,64,128]{2,1,0:T(8,128)(2,1)}) custom-call(s32[8,128]{1,0:T(8,128)S(1)} %get-tuple-element.17.idx_vec, bf16[4,32,32,128]{3,2,1,0:T(8,128)(2,1)} %get-tuple-element.18.hi_hbm, bf16[4,32,32,128]{3,2,1,0:T(8,128)(2,1)} %get-tuple-element.19.lo_hbm, ...), custom_call_target="tpu_custom_call" | custom-call | tf_op jit(solution)/shard_map/diffuse/pallas_call | solution.py:536
  68.4 10.8 %all-to-all-start.1 = ((bf16[128,64,128]{2,1,0:T(8,128)(2,1)}), bf16[128,64,128]{2,1,0:T(8,128)(2,1)S(1)}, u32[]{:S(2)}, u32[]{:S(2)}) async-start(bf16[128,64,128]{2,1,0:T(8,128)(2,1)} %get-tuple-element.26), calls=%async_computation.1 | async-start | bytes 4194304 | tf_op jit(solution)/shard_map/all_to_all | solution.py:683
  79.2 0.0 copy-start
  79.2 1.6 %copy-done = f32[4,32,32,128]{3,2,1,0:T(8,128)S(1)} copy-done((f32[4,32,32,128]{3,2,1,0:T(8,128)S(1)}, f32[4,32,32,128]{3,2,1,0:T(8,128)}, u32[]{:S(2)}) %copy-start) | copy-done | bytes 2097176
  80.8 5.8 %layout.1 = f32[2048,256]{1,0:T(8,128)} custom-call(f32[4,32,32,128]{3,2,1,0:T(8,128)S(1)} %copy-done), custom_call_target="tpu_custom_call" | custom-call | flops 8388608 | bytes 8388608 | tf_op jit(solution)/shard_map/layout/pallas_call | solution.py:593
  86.6 23.0 %all-to-all-done.1.tiles_ref = bf16[128,64,128]{2,1,0:T(8,128)(2,1)S(1)} async-done(((bf16[128,64,128]{2,1,0:T(8,128)(2,1)}), bf16[128,64,128]{2,1,0:T(8,128)(2,1)S(1)}, u32[]{:S(2)}, u32[]{:S(2)}) %all-to-all-start.1) | async-done | bytes 2097184 | tf_op jit(solution)/shard_map/all_to_all | solution.py:683
  109.6 8.3 %forward.1 = f32[12,8,128]{2,1,0:T(8,128)} custom-call(s32[156]{0:T(256)} %get-tuple-element.15.pos_hbm, bf16[128,64,128]{2,1,0:T(8,128)(2,1)S(1)} %all-to-all-done.1.tiles_ref, bf16[12,12,128,512]{3,2,1,0:T(8,128)(2,1)} %foot_hbm.3), custom_call_target="tpu_custom_call" | custom-call | tf_op jit(solution)/shard_map/forward/pallas_call | solution.py:666
  (1 shorter events, 0.0 us)
Async XLA Ops:
  8.5 11.0 %copy-start.1 = (f32[256,64]{0,1:T(8,128)S(1)}, f32[256,64]{0,1:T(8,128)}, u32[]{:S(2)}) copy-start(f32[256,64]{0,1:T(8,128)} %param.16) | copy-start | bytes 196612
  8.5 11.0 %copy-start.2 = (s32[256,64]{0,1:T(8,128)S(1)}, s32[256,64]{0,1:T(8,128)}, u32[]{:S(2)}) copy-start(s32[256,64]{0,1:T(8,128)} %param.17) | copy-start | bytes 196612
  8.5 44.2 %all-to-all-start = ((bf16[128,72,128]{2,1,0:T(8,128)(2,1)}), bf16[128,72,128]{2,1,0:T(8,128)(2,1)S(1)}, u32[]{:S(2)}, u32[]{:S(2)}) async-start(bf16[128,72,128]{2,1,0:T(8,128)(2,1)} %get-tuple-element.16), calls=%async_computation | async-start | bytes 4718592 | tf_op jit(solution)/shard_map/all_to_all | solution.py:683
  56.0 4.0 %collective-permute-start = (bf16[4,32,128]{2,1,0:T(8,128)(2,1)S(1)}, bf16[4,32,128]{2,1,0:T(8,128)(2,1)S(1)}, u32[]{:S(2)}, u32[]{:S(2)}) collective-permute-start(bf16[4,32,128]{2,1,0:T(8,128)(2,1)S(1)} %get-tuple-element.20), channel_id=1, source_target_pairs={{0,32},{64,96},{32,0},{96,64},{1,33},{65,97},{33,1},{97,65},{2,34}... | collective-permute-start | bytes 98312 | tf_op jit(solution)/shard_map/ppermute | solution.py:701
  56.7 3.3 %collective-permute-start.1 = (bf16[4,32,128]{2,1,0:T(8,128)(2,1)S(1)}, bf16[4,32,128]{2,1,0:T(8,128)(2,1)S(1)}, u32[]{:S(2)}, u32[]{:S(2)}) collective-permute-start(bf16[4,32,128]{2,1,0:T(8,128)(2,1)S(1)} %get-tuple-element.21), channel_id=1, source_target_pairs={{32,64},{64,32},{33,65},{65,33},{34,66},{66,34},{35,67},{67,35},{3... | collective-permute-start | bytes 98312 | tf_op jit(solution)/shard_map/ppermute | solution.py:702
  60.1 2.4 %collective-permute-start.2 = (bf16[9,32,128]{2,1,0:T(8,128)(2,1)S(1)}, bf16[9,32,128]{2,1,0:T(8,128)(2,1)S(1)}, u32[]{:S(2)}, u32[]{:S(2)}) collective-permute-start(bf16[9,32,128]{2,1,0:T(8,128)(2,1)S(1)} %get-tuple-element.24), channel_id=1, source_target_pairs={{1,2},{3,4},{5,6},{7,8},{9,10},{11,12},{13,14},{15,16},{17,18},{19... | collective-permute-start | bytes 221192 | tf_op jit(solution)/shard_map/ppermute | solution.py:704
  60.7 2.6 %collective-permute-start.3 = (bf16[9,32,128]{2,1,0:T(8,128)(2,1)S(1)}, bf16[9,32,128]{2,1,0:T(8,128)(2,1)S(1)}, u32[]{:S(2)}, u32[]{:S(2)}) collective-permute-start(bf16[9,32,128]{2,1,0:T(8,128)(2,1)S(1)} %get-tuple-element.25), channel_id=1, source_target_pairs={{0,1},{2,3},{4,5},{6,7},{8,9},{10,11},{12,13},{14,15},{16,17},{18,... | collective-permute-start | bytes 221192 | tf_op jit(solution)/shard_map/ppermute | solution.py:705
  68.4 41.2 %all-to-all-start.1 = ((bf16[128,64,128]{2,1,0:T(8,128)(2,1)}), bf16[128,64,128]{2,1,0:T(8,128)(2,1)S(1)}, u32[]{:S(2)}, u32[]{:S(2)}) async-start(bf16[128,64,128]{2,1,0:T(8,128)(2,1)} %get-tuple-element.26), calls=%async_computation.1 | async-start | bytes 4194304 | tf_op jit(solution)/shard_map/all_to_all | solution.py:683
  79.2 1.6 %copy-start = (f32[4,32,32,128]{3,2,1,0:T(8,128)S(1)}, f32[4,32,32,128]{3,2,1,0:T(8,128)}, u32[]{:S(2)}) copy-start(f32[4,32,32,128]{3,2,1,0:T(8,128)} %get-tuple-element.27.inc_ref) | copy-start | bytes 6291460
